TPU v7x, 128 devices: a whole 4x4x4 slice. The times are simulated.
128 devices in a mesh: seq: 32 (over x, z, core), head: 4 (over y).
Axes of the slice: x: 4, y: 4, z: 4, core: 2. Of those that a mesh axis runs over, the one named last changes fastest.
Arguments:
- values: bfloat16 [32768, 8192], P('seq', 'head'), may hold values from -0.0625 to 0.0625
- writes: bfloat16 [32768, 128], P('seq'), may hold values from -0.5 to 0.5
- reads: bfloat16 [32768, 128], P('seq'), may hold values from -0.5 to 0.5
- out_grad: bfloat16 [32768, 8192], P('seq', 'head'), may hold values from -0.375 to 0.375
- log_decay: float32 [128, 32768], P('head', 'seq'), may hold values from -2 to 0, as said below
- starting_head_state: float32 [128, 8192], P('head'), may hold values from -1.5 to 1.5
Outputs:
- values_grad: bfloat16 [32768, 8192], P('seq', 'head')
- writes_grad: float32 [32768, 128], P('seq')
- reads_grad: float32 [32768, 128], P('seq')
- initial_grad: float32 [128, 8192], P('head')
Inputs may be any that keep to these rules, and one draw needn't show every extreme that they name: `log_decay`: each entry is the logarithm of a head's decay factor at a position.
All inputs are finite; a program needn't handle non-finite values.
Results may differ from a plain program's by a relative error of at most 0.0013.
Values sent between devices are 32-bit elements; how exact they have to be, the bound alone decides.
A program may use at most 256 MiB of HBM per device.

v0:
```python
import jax
import jax.numpy as jnp
from jax import lax
from jax.sharding import PartitionSpec as P

HEAD_DIM = 64
D_STATE = 128


highest = lax.Precision.HIGHEST


def carried_in(part, axis, combine, identity, reverse):
    count = lax.axis_size(axis)
    place = lax.axis_index(axis)
    ahead = count - 1 - place if reverse else place
    gathered = jax.tree.map(lambda a: lax.all_gather(a, axis), part)
    state = jax.tree.map(lambda a, e: jnp.zeros_like(a) + jnp.asarray(e, a.dtype), part, identity)

    def one(turn, state):
        source = count - 1 - turn if reverse else turn
        return combine(
            state, jax.tree.map(lambda a: lax.dynamic_index_in_dim(a, source, 0, False), gathered)
        )

    return lax.fori_loop(0, ahead, one, state)


def forward_join(earlier, latter):
    return (earlier[0] + latter[0], jnp.exp(latter[0]) * earlier[1] + latter[1])


def backward_join(earlier, latter):
    return (earlier[0] + latter[0], latter[1] + jnp.exp(latter[0]) * earlier[1])


def per_device(values, writes, reads, out_grad, log_decay, starting_head_state):
    tokens = values.shape[0]
    head_count = log_decay.shape[0]
    block_size = min(512, tokens)
    block_count = tokens // block_size
    state_shape = (head_count, HEAD_DIM, D_STATE)
    flat_size = HEAD_DIM * D_STATE
    causal = lax.broadcasted_iota(jnp.int32, (block_size, block_size), 0) >= lax.broadcasted_iota(
        jnp.int32, (block_size, block_size), 1
    )
    blocks = []
    for block_index in range(block_count):
        first_row = block_index * block_size
        block_values = lax.slice_in_dim(values, first_row, first_row + block_size).reshape(
            block_size, head_count, HEAD_DIM
        )
        block_grads = lax.slice_in_dim(out_grad, first_row, first_row + block_size).reshape(
            block_size, head_count, HEAD_DIM
        )
        block_writes = lax.slice_in_dim(writes, first_row, first_row + block_size)
        block_reads = lax.slice_in_dim(reads, first_row, first_row + block_size)
        block_logs = lax.slice_in_dim(log_decay, first_row, first_row + block_size, axis=1)
        cumulative = jnp.cumsum(block_logs, axis=1)
        block_total = cumulative[:, -1]
        to_end = jnp.exp(block_total[:, None] - cumulative).T[:, :, None]
        from_start = jnp.exp(cumulative).T[:, :, None]
        log_gaps = cumulative[:, :, None] - cumulative[:, None, :]
        decay_mask = jnp.exp(jnp.where(causal[None], log_gaps, -1e30))
        intersections = jnp.einsum(
            "sn,in->si", block_reads, block_writes, preferred_element_type=jnp.float32
        )
        products = jnp.einsum(
            "shp,ihp->hsi", block_grads, block_values, preferred_element_type=jnp.float32
        )
        mixed_sums = jnp.sum(products * decay_mask, axis=0)
        values_wide = block_values.astype(jnp.float32)
        grads_wide = block_grads.astype(jnp.float32)
        writes_wide = block_writes.astype(jnp.float32)
        reads_wide = block_reads.astype(jnp.float32)
        interior_quantities = jnp.einsum(
            "hsi,shp->ihp", intersections[None] * decay_mask, grads_wide, precision=highest
        )
        inner_writes = jnp.einsum("si,sn->in", mixed_sums, reads_wide, precision=highest)
        inner_reads = jnp.einsum("si,in->sn", mixed_sums, writes_wide, precision=highest)
        rescaled_quantities = values_wide * to_end
        scaled_grads = grads_wide * from_start
        fresh_state = jnp.einsum("jhp,jn->hpn", rescaled_quantities, writes_wide, precision=highest)
        carried = jnp.einsum("shp,sn->hpn", scaled_grads, reads_wide, precision=highest)
        blocks.append(
            (
                block_total,
                to_end,
                writes_wide,
                rescaled_quantities,
                scaled_grads,
                interior_quantities,
                inner_writes,
                inner_reads,
                fresh_state,
                carried,
            )
        )
    local_state = jnp.zeros(state_shape, jnp.float32)
    total_log = jnp.zeros((head_count,), jnp.float32)
    for block_index in range(block_count):
        block_total = blocks[block_index][0]
        local_state = jnp.exp(block_total)[:, None, None] * local_state + blocks[block_index][8]
        total_log = total_log + block_total
    local_adjoint = jnp.zeros(state_shape, jnp.float32)
    for block_index in reversed(range(block_count)):
        block_total = blocks[block_index][0]
        local_adjoint = blocks[block_index][9] + jnp.exp(block_total)[:, None, None] * local_adjoint
    local_state = local_state.reshape(head_count, flat_size)
    local_adjoint = local_adjoint.reshape(head_count, flat_size)
    empty = (
        jnp.zeros((head_count, 1), jnp.float32),
        jnp.zeros((head_count, flat_size), jnp.float32),
    )
    prefix_log, prefix_state = carried_in(
        (total_log[:, None], local_state), "seq", forward_join, empty, False
    )
    ignored, after_device = carried_in(
        (total_log[:, None], local_adjoint), "seq", backward_join, empty, True
    )
    entering = prefix_state + jnp.exp(prefix_log) * starting_head_state
    initial_grad = lax.psum(jnp.exp(prefix_log) * local_adjoint, "seq")
    start_state = entering.reshape(state_shape)
    starts = []
    for block_index in range(block_count):
        starts.append(start_state)
        start_state = (
            jnp.exp(blocks[block_index][0])[:, None, None] * start_state + blocks[block_index][8]
        )
    after_end = after_device.reshape(state_shape)
    afters = [after_end] * block_count
    for block_index in reversed(range(block_count)):
        afters[block_index] = after_end
        after_end = (
            blocks[block_index][9] + jnp.exp(blocks[block_index][0])[:, None, None] * after_end
        )
    value_parts = []
    write_parts = []
    read_parts = []
    for block_index in range(block_count):
        (
            block_total,
            to_end,
            writes_wide,
            rescaled_quantities,
            scaled_grads,
            interior_quantities,
            inner_writes,
            inner_reads,
            fresh_state,
            carried,
        ) = blocks[block_index]
        outer_values = (
            jnp.einsum("in,hpn->ihp", writes_wide, afters[block_index], precision=highest) * to_end
        )
        value_parts.append(
            (interior_quantities + outer_values)
            .reshape(block_size, head_count * HEAD_DIM)
            .astype(jnp.bfloat16)
        )
        write_parts.append(
            inner_writes
            + jnp.einsum("ihp,hpn->in", rescaled_quantities, afters[block_index], precision=highest)
        )
        read_parts.append(
            inner_reads
            + jnp.einsum("shp,hpn->sn", scaled_grads, starts[block_index], precision=highest)
        )
    values_grad = jnp.concatenate(value_parts, axis=0)
    writes_local = jnp.concatenate(write_parts, axis=0)
    reads_local = jnp.concatenate(read_parts, axis=0)
    writes_grad, reads_grad = lax.psum((writes_local, reads_local), "head")
    return (values_grad, writes_grad, reads_grad, initial_grad)


def solution(mesh):
    in_specs = (
        P("seq", "head"),
        P("seq", None),
        P("seq", None),
        P("seq", "head"),
        P("head", "seq"),
        P("head", None),
    )
    out_specs = (P("seq", "head"), P("seq", None), P("seq", None), P("head", None))
    return jax.shard_map(
        per_device, mesh=mesh, in_specs=in_specs, out_specs=out_specs, check_vma=False
    )
```

profile of v0, /device:TPU:0, one launch (start us, length us, event | category | flops | bytes accessed | tf_op | source)
XLA Modules:
  0.0 539.7 jit_solution(1974260773346399867)
XLA Ops:
  13.3 4.8 fusion.76
  18.1 2.9 copy.60
  21.1 4.6 copy.53
  25.7 3.8 fusion.27
  29.5 3.9 fusion.38
  33.4 2.4 all_gather_reshape.6
  36.1 4.8 fusion.75
  41.0 4.0 copy.61
  45.0 4.0 copy.58
  48.9 4.0 fusion.21
  53.9 4.8 fusion.41
  61.3 4.3 bitcast_multiply_fusion.1
  65.5 2.6 bitcast_multiply_fusion
  69.7 70.5 %all-reduce = f32[1024]{0:T(1024)S(1)} all-reduce(f32[1024]{0:T(1024)S(1)} %dynamic-update-slice), channel_id=2, replica_groups=mesh['seq'=32,'head'=4] {'seq'}, use_global_device_ids=true, to_apply=%add | all-reduce | flops 1024 | bytes 8192
  144.9 14.0 %multiply_reduce_fusion = f32[512,512]{1,0:T(8,128)} fusion(f32[32,512]{1,0:T(8,128)} %copy-done.28, pred[512,512]{1,0:T(8,128)(4,1)S(1)} %iota_compare_fusion, bf16[512,32,64]{0,2,1:T(8,128)(2,1)} %bitcast.143, bf16[512,32,64]{0,2,1:T(8,128)(2,1)} %bitcast.150), kind=kOutput, calls=%fused_computation.6 | convolution fusion | flops 1107034112 | bytes 5570560 | tf_op jit(solution)/shard_map/shp,ihp->hsi/dot_general | solution.py:68
  158.9 11.7 %multiply_reduce_fusion.1 = f32[512,512]{1,0:T(8,128)} fusion(f32[32,512]{1,0:T(8,128)S(1)} %copy-done.26, pred[512,512]{1,0:T(8,128)(4,1)S(1)} %iota_compare_fusion, bf16[512,32,64]{0,2,1:T(8,128)(2,1)S(1)} %bitcast.140, bf16[512,32,64]{0,2,1:T(8,128)(2,1)S(1)} %bitcast.148), kind=kOutput, calls=%fused_computation.7 | convolution fusion | flops 1107034112 | bytes 5570560 | tf_op jit(solution)/shard_map/shp,ihp->hsi/dot_general | solution.py:68
  170.6 48.5 %while.26 = (s32[]{:T(128)}, f32[32,8192]{1,0:T(8,128)S(1)}, s32[]{:T(128)}, f32[32,32,8192]{2,1,0:T(8,128)}, f32[32,32,1]{1,2,0:T(1,128)S(1)}, /*index=5*/s32[]{:T(128)}, s32[]{:T(128)}, s32[]{:T(128)}, s32[]{:T(128)}) while((s32[]{:T(128)}, f32[32,8192]{1,0:T(8,128)S(1)}, s32[]{:T(128)}, f32[32,32,8192]{2,1,0:T(8,128)}, ...), condition=%wide.region_5.6_spmd, body=%wide.region_4.5_spmd.sunk | while | flops 524294 | bytes 3146267 | solution.py:26
  219.4 9.2 %fusion.45 = f32[512,128]{1,0:T(8,128)} fusion(bf16[512,32,64]{0,2,1:T(8,128)(2,1)} %bitcast.147, f32[512,32]{0,1:T(8,128)S(1)} %copy-done.22, f32[32,64,128]{2,1,0:T(8,128)S(1)} %fusion.27, f32[32,64,128]{2,1,0:T(8,128)S(1)} %bitcast.135, f32[32]{0:T(128)} %copy-done.29), kind=kOutput, calls=%fused_computation.56 | convolution fusion | flops 1613234176 | bytes 4522112 | tf_op jit(solution)/shard_map/ihp,hpn->in/dot_general | solution.py:163
  228.6 7.6 %convolution_bitcast_fusion.1 = f32[512,128]{1,0:T(8,128)} fusion(f32[512,32,64]{0,2,1:T(8,128)S(1)} %bitcast.152, f32[32,64,128]{2,1,0:T(8,128)S(1)} %bitcast.136), kind=kOutput, calls=%fused_computation.54 | convolution fusion | flops 1610612736 | bytes 5505024 | tf_op jit(solution)/shard_map/ihp,hpn->in/dot_general | solution.py:163
  236.2 3.8 fusion.51
  240.1 28.4 %all-gather.6.cloned.1.call-done = f32[32,32,8192]{2,1,0:T(8,128)} async-done(((f32[1,32,8192]{2,1,0:T(8,128)}), f32[32,32,8192]{2,1,0:T(8,128)}) %all-gather.6.cloned.1.call-update) | async-done | bytes 33554448 | tf_op jit(solution)/shard_map/all_gather | solution.py:17
  270.3 3.0 bitcast_multiply_fusion.4
  273.5 6.8 %fusion.44 = f32[512,128]{1,0:T(8,128)S(1)} fusion(bf16[512,32,64]{0,2,1:T(8,128)(2,1)S(1)} %bitcast.144, f32[512,32]{0,1:T(8,128)S(1)} %copy-done.23, f32[32,64,128]{2,1,0:T(8,128)S(1)} %copy-done.9, f32[32,64,128]{2,1,0:T(8,128)S(1)} %bitcast.154, f32[32]{0:T(128)S(1)} %copy-done.32), kind=kOutput, calls=%fused_computation.55 | convolution fusion | flops 1613234176 | bytes 4522112 | tf_op jit(solution)/shard_map/shp,hpn->sn/dot_general | solution.py:167
  283.4 7.0 %convolution_bitcast_fusion = f32[512,128]{1,0:T(8,128)S(1)} fusion(f32[512,32,64]{0,2,1:T(8,128)S(1)} %bitcast.151, f32[32,64,128]{2,1,0:T(8,128)S(1)} %bitcast.155), kind=kOutput, calls=%fused_computation.53 | convolution fusion | flops 1610612736 | bytes 5505024 | tf_op jit(solution)/shard_map/shp,hpn->sn/dot_general | solution.py:167
  293.5 22.8 %fusion.15 = bf16[512,32,64]{0,2,1:T(8,128)(2,1)} fusion(f32[32,64,512]{2,1,0:T(8,128)} %fusion.51, bf16[512,32,64]{0,2,1:T(8,128)(2,1)S(1)} %bitcast.145, f32[32,512]{1,0:T(8,128)} %copy-done.28, f32[512,512]{1,0:T(8,128)} %fusion.58, pred[512,512]{1,0:T(8,128)(4,1)} %copy-done.24, f32[512,32]{0,1:T(8,128)S(1)} %get-tuple-element.160), kind=kOutput, calls=%fused_computation.29 | convolution fusion | flops 6470762496 | bytes 9830400 | tf_op jit(solution)/shard_map/hsi,shp->ihp/dot_general | solution.py:76
  318.0 5.1 fusion.49
  323.1 22.6 %fusion.17 = bf16[512,32,64]{0,2,1:T(8,128)(2,1)} fusion(f32[32,64,512]{2,1,0:T(8,128)} %fusion.49, bf16[512,32,64]{0,2,1:T(8,128)(2,1)S(1)} %bitcast.141, f32[32,512]{1,0:T(8,128)S(1)} %copy-done.27, f32[512,512]{1,0:T(8,128)} %fusion.63, pred[512,512]{1,0:T(8,128)(4,1)} %copy-done.24, f32[512,32]{0,1:T(8,128)S(1)} %copy-done.22), kind=kOutput, calls=%fused_computation.32 | convolution fusion | flops 6470762496 | bytes 9830400 | tf_op jit(solution)/shard_map/hsi,shp->ihp/dot_general | solution.py:76
  345.7 2.9 copy.57
  348.6 4.0 copy.56
  352.6 4.1 pad_maximum_fusion
  356.7 121.6 %all-reduce.5.cloned.1.call-done = f32[32,8192]{1,0:T(8,128)} async-done(((f32[32,8192]{1,0:T(8,128)}), f32[32,8192]{1,0:T(8,128)}) %all-reduce.5.cloned.1.call-update) | async-done | bytes 1048592 | tf_op jit(solution)/shard_map/psum | solution.py:122
  478.3 48.5 %all-reduce.7.cloned.1.call-done = (f32[1024,128]{1,0:T(8,128)}, f32[1024,128]{1,0:T(8,128)}) async-done(((f32[1024,128]{1,0:T(8,128)}, f32[1024,128]{1,0:T(8,128)}), (f32[1024,128]{1,0:T(8,128)}, f32[1024,128]{1,0:T(8,128)})) %all-reduce.7.cloned.1.call-update) | async-done | bytes 1048592 | tf_op jit(solution)/shard_map/psum | solution.py:172
  (180 shorter events, 78.6 us)
Async XLA Ops:
  7.2 163.4 %all-gather.4.cloned.1.call-start = ((), (), s32[]{:S(2)}) async-start(), calls=%async_computation | async-start | bytes 34603008 | tf_op jit(solution)/shard_map/all_gather | solution.py:17
  9.6 8.5 %copy-start.25 = (f32[32,512]{1,0:T(8,128)}, f32[32,512]{1,0:T(8,128)S(1)}, u32[]{:S(2)}) copy-start(f32[32,512]{1,0:T(8,128)S(1)} %copy_bitcast_fusion.1) | copy-start | bytes 196612
  11.1 7.1 %copy-start.28 = (f32[32,512]{1,0:T(8,128)}, f32[32,512]{1,0:T(8,128)S(1)}, u32[]{:S(2)}) copy-start(f32[32,512]{1,0:T(8,128)S(1)} %copy_bitcast_fusion) | copy-start | bytes 196612
  12.5 40.4 %copy-start.29 = (f32[32]{0:T(128)}, f32[32]{0:T(128)S(1)}, u32[]{:S(2)}) copy-start(f32[32]{0:T(128)S(1)} %get-tuple-element.166) | copy-start | bytes 388
  13.3 16.2 %copy-start.31 = (f32[32]{0:T(128)}, f32[32]{0:T(128)S(1)}, u32[]{:S(2)}) copy-start(f32[32]{0:T(128)S(1)} %get-tuple-element.165) | copy-start | bytes 388
  18.1 7.6 %copy-start.14 = (bf16[1024,128]{1,0:T(8,128)(2,1)S(1)}, bf16[1024,128]{1,0:T(8,128)(2,1)}, u32[]{:S(2)}) copy-start(bf16[1024,128]{1,0:T(8,128)(2,1)} %param.12) | copy-start | bytes 786436
  21.1 137.8 %copy-start = (bf16[512,2048]{0,1:T(8,128)(2,1)}, bf16[512,2048]{0,1:T(8,128)(2,1)S(1)}, u32[]{:S(2)}) copy-start(bf16[512,2048]{0,1:T(8,128)(2,1)S(1)} %copy.60) | copy-start | bytes 6291460
  29.5 189.9 %copy-start.5 = (f32[32,64,128]{2,1,0:T(8,128)}, f32[32,64,128]{2,1,0:T(8,128)S(1)}, u32[]{:S(2)}) copy-start(f32[32,64,128]{2,1,0:T(8,128)S(1)} %fusion.27) | copy-start | bytes 3145732
  35.9 232.6 %all-gather.6.cloned.1.call-start = ((), (), s32[]{:S(2)}) async-start(), calls=%async_computation.1 | async-start | bytes 34603008 | tf_op jit(solution)/shard_map/all_gather | solution.py:17
  41.0 7.9 %copy-start.13 = (bf16[1024,128]{1,0:T(8,128)(2,1)S(1)}, bf16[1024,128]{1,0:T(8,128)(2,1)}, u32[]{:S(2)}) copy-start(bf16[1024,128]{1,0:T(8,128)(2,1)} %param.11) | copy-start | bytes 786436
  61.2 417.1 %all-reduce.5.cloned.1.call-start = ((), (), s32[]{:S(2)}) async-start(), calls=%async_computation.2 | async-start | bytes 2097152 | tf_op jit(solution)/shard_map/psum | solution.py:122
  140.4 18.5 %copy-start.24 = (pred[512,512]{1,0:T(8,128)(4,1)}, pred[512,512]{1,0:T(8,128)(4,1)S(1)}, u32[]{:S(2)}) copy-start(pred[512,512]{1,0:T(8,128)(4,1)S(1)} %iota_compare_fusion) | copy-start | bytes 786436
  144.9 14.0 %copy-start.4 = (bf16[512,2048]{0,1:T(8,128)(2,1)S(1)}, bf16[512,2048]{0,1:T(8,128)(2,1)}, u32[]{:S(2)}) copy-start(bf16[512,2048]{0,1:T(8,128)(2,1)} %copy.58) | copy-start | bytes 6291460
  144.9 14.0 %copy-start.26 = (f32[32,512]{1,0:T(8,128)S(1)}, f32[32,512]{1,0:T(8,128)}, u32[]{:S(2)}) copy-start(f32[32,512]{1,0:T(8,128)} %copy-done.25) | copy-start | bytes 196612
  170.6 48.8 %copy-start.22 = (f32[512,32]{0,1:T(8,128)S(1)}, f32[512,32]{0,1:T(8,128)}, u32[]{:S(2)}) copy-start(f32[512,32]{0,1:T(8,128)} %get-tuple-element.158) | copy-start | bytes 196612
  219.2 9.4 %copy-start.7 = (f32[512,2048]{0,1:T(8,128)S(1)}, f32[512,2048]{0,1:T(8,128)}, u32[]{:S(2)}) copy-start(f32[512,2048]{0,1:T(8,128)} %bitcast_multiply_fusion.1) | copy-start | bytes 12582916
  269.1 4.4 copy-start.2
  273.3 7.0 %copy-start.12 = (f32[512,512]{1,0:T(8,128)S(1)}, f32[512,512]{1,0:T(8,128)}, u32[]{:S(2)}) copy-start(f32[512,512]{1,0:T(8,128)} %multiply_reduce_fusion) | copy-start | bytes 3145732
  273.3 7.0 %copy-start.15 = (bf16[1024,128]{1,0:T(8,128)(2,1)S(1)}, bf16[1024,128]{1,0:T(8,128)(2,1)}, u32[]{:S(2)}) copy-start(bf16[1024,128]{1,0:T(8,128)(2,1)} %param.12) | copy-start | bytes 786436
  273.3 7.0 %copy-start.21 = (f32[512,128]{1,0:T(8,128)S(1)}, f32[512,128]{1,0:T(8,128)}, u32[]{:S(2)}) copy-start(f32[512,128]{1,0:T(8,128)} %convolution_bitcast_fusion.1) | copy-start | bytes 786436
  273.5 9.9 %copy-start.6 = (f32[512,2048]{0,1:T(8,128)S(1)}, f32[512,2048]{0,1:T(8,128)}, u32[]{:S(2)}) copy-start(f32[512,2048]{0,1:T(8,128)} %bitcast_multiply_fusion) | copy-start | bytes 12582916
  280.3 10.0 %copy-start.11 = (f32[512,512]{1,0:T(8,128)S(1)}, f32[512,512]{1,0:T(8,128)}, u32[]{:S(2)}) copy-start(f32[512,512]{1,0:T(8,128)} %multiply_reduce_fusion.1) | copy-start | bytes 3145732
  280.3 10.0 %copy-start.16 = (f32[512,128]{1,0:T(8,128)S(1)}, f32[512,128]{1,0:T(8,128)}, u32[]{:S(2)}) copy-start(f32[512,128]{1,0:T(8,128)} %fusion.45) | copy-start | bytes 786436
  283.4 10.1 %copy-start.3 = (bf16[512,2048]{0,1:T(8,128)(2,1)S(1)}, bf16[512,2048]{0,1:T(8,128)(2,1)}, u32[]{:S(2)}) copy-start(bf16[512,2048]{0,1:T(8,128)(2,1)} %copy.53) | copy-start | bytes 6291460
  293.4 24.6 %copy-start.30 = (f32[32]{0:T(128)S(1)}, f32[32]{0:T(128)}, u32[]{:S(2)}) copy-start(f32[32]{0:T(128)} %copy-done.29) | copy-start | bytes 388
  293.4 233.3 %all-reduce.7.cloned.1.call-start = ((), (), s32[]{:S(2)}) async-start(), calls=%async_computation.3 | async-start | bytes 2097152 | tf_op jit(solution)/shard_map/psum | solution.py:172
  293.5 22.8 %copy-start.18 = (f32[512,128]{1,0:T(8,128)S(1)}, f32[512,128]{1,0:T(8,128)}, u32[]{:S(2)}) copy-start(f32[512,128]{1,0:T(8,128)} %convolution_add_fusion.2) | copy-start | bytes 786436
  293.5 22.8 %copy-start.20 = (f32[512,128]{1,0:T(8,128)S(1)}, f32[512,128]{1,0:T(8,128)}, u32[]{:S(2)}) copy-start(f32[512,128]{1,0:T(8,128)} %convolution_add_fusion.3) | copy-start | bytes 786436
  293.5 23.7 %copy-start.17 = (f32[512,128]{1,0:T(8,128)S(1)}, f32[512,128]{1,0:T(8,128)}, u32[]{:S(2)}) copy-start(f32[512,128]{1,0:T(8,128)} %convolution_add_fusion) | copy-start | bytes 786436
  293.5 23.6 %copy-start.19 = (f32[512,128]{1,0:T(8,128)S(1)}, f32[512,128]{1,0:T(8,128)}, u32[]{:S(2)}) copy-start(f32[512,128]{1,0:T(8,128)} %convolution_add_fusion.1) | copy-start | bytes 786436
  317.2 5.9 %copy-start.1 = (bf16[512,2048]{0,1:T(8,128)(2,1)S(1)}, bf16[512,2048]{0,1:T(8,128)(2,1)}, u32[]{:S(2)}) copy-start(bf16[512,2048]{0,1:T(8,128)(2,1)} %copy-done) | copy-start | bytes 6291460
  317.2 6.0 %copy-start.27 = (f32[32,512]{1,0:T(8,128)S(1)}, f32[32,512]{1,0:T(8,128)}, u32[]{:S(2)}) copy-start(f32[32,512]{1,0:T(8,128)} %copy-done.25) | copy-start | bytes 196612
  (6 other events, 17.9 us)
Sparse Core Ops, SparseCore 0:
  36.0 117.0 all-gather.3
  155.4 113.0 all-gather.5
  293.5 184.7 all-reduce.4
  481.3 45.4 all-reduce.6
where the time goes:
time: 547 us; the launch traced here: 540 us
  waiting for transfers between devices  199 us (36%)
  matrix products  137 us (25%)
  blocking collectives  70.5 us (13%)
  other arithmetic  67.2 us (12%)
  local copies, waits for them, and re-layouts  48.8 us (9%)
  between operations  15.3 us (3%)
    psum x1, waiting for transfers between devices, per_device(): initial_grad = lax.psum(jnp.exp(prefix_log) * local_adjoint, 'seq')  122 us
    unnamed x1, blocking collectives  70.5 us
    psum x1, waiting for transfers between devices, per_device(): writes_grad, reads_grad = lax.psum((writes_local, reads_local), 'head')  48.5 us
    add x31, other arithmetic, backward_join(): return (earlier[0] + latter[0], latter[1] + jnp.exp(latter[0]) * earlier[1])  46.8 us
    dot_general x2, matrix products, per_device(): jnp.einsum('hsi,shp->ihp', intersections[None] * decay_mask, grads_wide,...  45.4 us
    all_gather x2, waiting for transfers between devices, carried_in(): gathered = jax.tree.map(lambda a: lax.all_gather(a, axis), part)  28.4 us
    dot_general x2, matrix products, per_device(): jnp.einsum('shp,ihp->hsi', block_grads, block_values, preferred_element_t...  25.7 us
    dot_general x2, matrix products, per_device(): jnp.einsum('ihp,hpn->in', rescaled_quantities, afters[block_index], preci...  16.8 us
  transfers between devices with their start and end apart: 4, of which 3 were waited for; matrix products, arithmetic and copies ran while one was open for 36% of the time, Pallas kernels for 0%

commit v1 on v0

v1 whole, which is shorter than its diff:
```python
import functools

import jax
import jax.numpy as jnp
from jax import lax
from jax.experimental import pallas as pl
from jax.experimental.pallas import tpu as pltpu
from jax.sharding import PartitionSpec as P

HEAD_DIM = 64
D_STATE = 128
CHUNK = 128

MESH = pl.DeviceIdType.MESH
F32 = jnp.float32
BF16 = jnp.bfloat16
NN = (((1,), (0,)), ((), ()))
NT = (((1,), (1,)), ((), ()))
TN = (((0,), (0,)), ((), ()))
VMEM_LIMIT = 56 * 1024 * 1024


def dot(a, b, dims=NN):
    return lax.dot_general(a, b, dims, preferred_element_type=F32)


def split2(a):
    hi = a.astype(BF16)
    return hi, (a - hi.astype(F32)).astype(BF16)


def split3(a):
    hi = a.astype(BF16)
    rest = a - hi.astype(F32)
    mid = rest.astype(BF16)
    return hi, mid, (rest - mid.astype(F32)).astype(BF16)


def iota(shape, dim):
    return lax.broadcasted_iota(jnp.int32, shape, dim)


def spread_matrix(copies, heads):
    shape = (copies * heads, heads * HEAD_DIM)
    row = lax.rem(iota(shape, 0), heads)
    return (row == iota(shape, 1) // HEAD_DIM).astype(F32).astype(BF16)


def spread2(a, matrix):
    return dot(jnp.concatenate(split2(a), axis=1), matrix)


def local_kernel(values, writes, grads, reads, logs, state, adjoint, total, later, sooner):
    step = pl.program_id(0)
    tokens = values.shape[0]
    heads = logs.shape[0]
    steps = pl.num_programs(0)
    spread = spread_matrix(2, heads)
    first = pl.multiple_of(step * tokens, tokens)

    @pl.when(step == 0)
    def _():
        state[...] = jnp.zeros_like(state)
        adjoint[...] = jnp.zeros_like(adjoint)
        size = 256
        row, col = iota((size, size), 0), iota((size, size), 1)
        after = (col > row).astype(F32).astype(BF16)
        upto = (col <= row).astype(F32).astype(BF16)
        ones = jnp.ones((8, size), BF16)
        count = later.shape[0] // size
        parts = [split3(logs[:, k * size : (k + 1) * size]) for k in range(count)]
        sums = [sum(dot(ones, p, NT) for p in part) for part in parts]
        before = jnp.zeros((1, heads), F32)
        for k in range(count):
            sooner[k * size : (k + 1) * size, :] = jnp.exp(sum(dot(upto, p, NT) for p in parts[k]) + before)
            before = before + sums[k][:1]
        behind = jnp.zeros((1, heads), F32)
        for k in reversed(range(count)):
            later[k * size : (k + 1) * size, :] = jnp.exp(sum(dot(after, p, NT) for p in parts[k]) + behind)
            behind = behind + sums[k][:1]
        matrix = spread[:heads]
        whole = jnp.broadcast_to(before, (8, heads))
        total[...] = sum(dot(p, matrix) for p in split3(whole))

    rows = pl.ds(first, tokens)
    scaled = values[...].astype(F32) * spread2(later[rows, :], spread)
    hi, lo = split2(scaled)
    state[...] += dot(writes[...], hi, TN) + dot(writes[...], lo, TN)
    scaled = grads[...].astype(F32) * spread2(sooner[rows, :], spread)
    hi, lo = split2(scaled)
    adjoint[...] += dot(reads[...], hi, TN) + dot(reads[...], lo, TN)


def local_part(values, writes, reads, grads, logs):
    tokens, width = values.shape
    heads = logs.shape[0]
    size = 256
    wide = pl.BlockSpec((size, width), lambda k: (k, 0))
    thin = pl.BlockSpec((size, D_STATE), lambda k: (k, 0))
    whole = lambda shape: pl.BlockSpec(shape, lambda k: (0, 0))
    return pl.pallas_call(
        local_kernel,
        grid=(tokens // size,),
        in_specs=[wide, thin, wide, thin, whole((heads, tokens))],
        out_specs=[whole((D_STATE, width)), whole((D_STATE, width)), whole((8, width))],
        out_shape=[
            jax.ShapeDtypeStruct((D_STATE, width), F32),
            jax.ShapeDtypeStruct((D_STATE, width), F32),
            jax.ShapeDtypeStruct((8, width), F32),
        ],
        scratch_shapes=[pltpu.VMEM((tokens, heads), F32), pltpu.VMEM((tokens, heads), F32)],
        compiler_params=pltpu.CompilerParams(vmem_limit_bytes=VMEM_LIMIT),
        cost_estimate=pl.CostEstimate(flops=2 * 2**30, bytes_accessed=12 * 2**20, transcendentals=0),
        name="local_part",
    )(values, writes, grads, reads, logs)


def scan_kernel(
    state, adjoint, total, start, entering, leaving, initial,
    near_state, near_adjoint, near_total, outgoing, incoming, replies, answers, mine, theirs,
    near_send, near_recv, out_send, out_recv, back_send, back_recv, last_send, last_recv,
):
    chips = incoming.shape[0]
    half = D_STATE // 2
    seq = lax.axis_index("seq")
    chip = seq // 2
    core = lax.rem(seq, 2)
    partner = {"seq": chip * 2 + 1 - core}
    lanes = 2 * HEAD_DIM

    barrier = pltpu.get_barrier_semaphore()
    for turn in range(1, chips):
        other = lax.rem(chip + turn, chips)
        pl.semaphore_signal(barrier, inc=1, device_id={"seq": other * 2 + core}, device_id_type=MESH)
    pl.semaphore_signal(barrier, inc=1, device_id=partner, device_id_type=MESH)
    pl.semaphore_wait(barrier, chips)

    own = pl.ds(pl.multiple_of(core * half, half), half)
    others = pl.ds(pl.multiple_of((1 - core) * half, half), half)
    nears = []
    for k, (source, target) in enumerate(
        ((state.at[others, :], near_state), (adjoint.at[others, :], near_adjoint), (total, near_total))
    ):
        copy = pltpu.make_async_remote_copy(
            src_ref=source, dst_ref=target, send_sem=near_send.at[k], recv_sem=near_recv.at[k],
            device_id=partner, device_id_type=MESH,
        )
        copy.start()
        nears.append(copy)
    for copy in nears:
        copy.wait()

    is_first = core == 0
    outs = []
    for turn in range(chips):
        target = lax.rem(chip + turn, chips)
        cols = pl.ds(pl.multiple_of(target * lanes, lanes), lanes)
        own_log, near_log = total[:, cols], near_total[:, cols]
        log_first = jnp.where(is_first, own_log, near_log)
        log_second = jnp.where(is_first, near_log, own_log)
        own_state, far_state = state[own, cols], near_state[:, cols]
        own_adjoint, far_adjoint = adjoint[own, cols], near_adjoint[:, cols]
        state_first = jnp.where(is_first, own_state, far_state)
        state_second = jnp.where(is_first, far_state, own_state)
        adjoint_first = jnp.where(is_first, own_adjoint, far_adjoint)
        adjoint_second = jnp.where(is_first, far_adjoint, own_adjoint)
        joined_state = jnp.exp(log_second[:1]) * state_first + state_second
        joined_adjoint = adjoint_first + jnp.exp(log_first[:1]) * adjoint_second
        place = incoming.at[chip] if turn == 0 else outgoing.at[target]
        place[0:half, :] = joined_state
        place[half : 2 * half, :] = joined_adjoint
        place[2 * half :, :] = log_first + log_second
        if turn:
            copy = pltpu.make_async_remote_copy(
                src_ref=outgoing.at[target], dst_ref=incoming.at[chip],
                send_sem=out_send.at[turn], recv_sem=out_recv.at[chip],
                device_id={"seq": target * 2 + core}, device_id_type=MESH,
            )
            copy.start()
            outs.append(copy)
    for turn in range(1, chips):
        source = lax.rem(chip + turn, chips)
        pltpu.make_async_remote_copy(
            src_ref=outgoing.at[source], dst_ref=incoming.at[source],
            send_sem=out_send.at[turn], recv_sem=out_recv.at[source],
            device_id={"seq": source * 2 + core}, device_id_type=MESH,
        ).wait_recv()

    carry = start[...]
    for k in range(chips):
        replies[k, 0:half, :] = carry
        carry = jnp.exp(incoming[k, 2 * half : 2 * half + 1, :]) * carry + incoming[k, 0:half, :]
    carry = jnp.zeros((half, lanes), F32)
    for k in reversed(range(chips)):
        replies[k, half:, :] = carry
        carry = jnp.exp(incoming[k, 2 * half : 2 * half + 1, :]) * carry + incoming[k, half : 2 * half, :]
    initial[...] = carry

    backs = []
    for turn in range(1, chips):
        target = lax.rem(chip + turn, chips)
        copy = pltpu.make_async_remote_copy(
            src_ref=replies.at[target], dst_ref=answers.at[chip],
            send_sem=back_send.at[turn], recv_sem=back_recv.at[chip],
            device_id={"seq": target * 2 + core}, device_id_type=MESH,
        )
        copy.start()
        backs.append(copy)
    for turn in range(chips):
        source = lax.rem(chip + turn, chips)
        if turn:
            pltpu.make_async_remote_copy(
                src_ref=replies.at[source], dst_ref=answers.at[source],
                send_sem=back_send.at[turn], recv_sem=back_recv.at[source],
                device_id={"seq": source * 2 + core}, device_id_type=MESH,
            ).wait_recv()
            answer = answers.at[source]
        else:
            answer = replies.at[chip]
        cols = pl.ds(pl.multiple_of(source * lanes, lanes), lanes)
        came, goes = answer[0:half, :], answer[half:, :]
        own_log, near_log = total[:1, cols], near_total[:1, cols]
        moved_state = jnp.where(
            is_first, jnp.exp(own_log) * came + state[own, cols], jnp.exp(near_log) * came + near_state[:, cols]
        )
        moved_adjoint = jnp.where(
            is_first, jnp.exp(near_log) * goes + near_adjoint[:, cols], jnp.exp(own_log) * goes + adjoint[own, cols]
        )
        mine[0, :, cols] = jnp.where(is_first, came, moved_state)
        mine[1, :, cols] = jnp.where(is_first, moved_adjoint, goes)
        theirs[0, :, cols] = jnp.where(is_first, moved_state, came)
        theirs[1, :, cols] = jnp.where(is_first, goes, moved_adjoint)

    lasts = []
    for k, target in enumerate((entering, leaving)):
        copy = pltpu.make_async_remote_copy(
            src_ref=theirs.at[k], dst_ref=target.at[own, :], send_sem=last_send.at[k], recv_sem=last_recv.at[k],
            device_id=partner, device_id_type=MESH,
        )
        copy.start()
        lasts.append(copy)
    entering[own, :] = mine[0]
    leaving[own, :] = mine[1]
    for copy in outs + backs:
        copy.wait_send()
    for copy in lasts:
        copy.wait()


def scan_part(state, adjoint, total, start, chips):
    width = state.shape[1]
    half = D_STATE // 2
    lanes = 2 * HEAD_DIM
    vmem = pl.BlockSpec(memory_space=pltpu.VMEM)
    dma = pltpu.SemaphoreType.DMA
    return pl.pallas_call(
        scan_kernel,
        in_specs=[vmem] * 4,
        out_specs=[vmem] * 3,
        out_shape=[
            jax.ShapeDtypeStruct((D_STATE, width), F32),
            jax.ShapeDtypeStruct((D_STATE, width), F32),
            jax.ShapeDtypeStruct((half, lanes), F32),
        ],
        scratch_shapes=[
            pltpu.VMEM((half, width), F32),
            pltpu.VMEM((half, width), F32),
            pltpu.VMEM((8, width), F32),
            pltpu.VMEM((chips, 2 * half + 8, lanes), F32),
            pltpu.VMEM((chips, 2 * half + 8, lanes), F32),
            pltpu.VMEM((chips, 2 * half, lanes), F32),
            pltpu.VMEM((chips, 2 * half, lanes), F32),
            pltpu.VMEM((2, half, width), F32),
            pltpu.VMEM((2, half, width), F32),
            dma((3,)), dma((3,)), dma((chips,)), dma((chips,)), dma((chips,)), dma((chips,)), dma((2,)), dma((2,)),
        ],
        compiler_params=pltpu.CompilerParams(collective_id=0, has_side_effects=True, vmem_limit_bytes=VMEM_LIMIT),
        cost_estimate=pl.CostEstimate(flops=2**22, bytes_accessed=5 * 2**20, transcendentals=0),
        name="scan_part",
    )(state, adjoint, total, start)


def gradient_kernel(
    values, writes, grads, reads, logs, entering, leaving, values_grad, writes_grad, reads_grad,
    now, scaled_hi, scaled_lo, carried, inner, inner_writes, ends, sums,
):
    step = pl.program_id(0)
    steps = pl.num_programs(0)
    count = steps // 2
    size, width = values.shape
    heads = logs.shape[0]
    pairs = heads // 2
    lanes = 2 * HEAD_DIM
    spread = spread_matrix(2, heads)

    @pl.when(step == 0)
    def _():
        now[...] = entering[...]

    @pl.when(step == count)
    def _():
        now[...] = leaving[...]

    @pl.when(step < count)
    def _():
        row, col = iota((size, size), 0), iota((size, size), 1)
        upto = (col <= row).astype(F32).astype(BF16)
        chunk_logs = logs[:, pl.ds(pl.multiple_of(step * size, size), size)]
        parts = split3(chunk_logs)
        by_row = sum(dot(upto, p, NT) for p in parts)
        by_col = sum(dot(p, upto, NT) for p in parts)
        last = by_row[size - 1 :, :]
        to_end = jnp.exp(last - by_row)
        sums[step, :, :] = sum(dot(p, spread[:heads]) for p in split3(jnp.broadcast_to(last, (8, heads))))
        ends[step, :, :] = to_end
        growth = jnp.exp(sums[step, 0:1, :])
        x, g, b, c = values[...], grads[...], writes[...], reads[...]

        x_hi, x_lo = split2(x.astype(F32) * spread2(to_end, spread))
        g_hi, g_lo = split2(g.astype(F32) * spread2(jnp.exp(by_row), spread))
        scaled_hi[step, :, :] = x_hi
        scaled_lo[step, :, :] = x_lo
        carried[step, :, :] = dot(c, g_hi, TN) + dot(c, g_lo, TN)
        s_hi, s_lo = split2(now[...])
        outer = dot(g_hi, s_hi, NT) + dot(g_hi, s_lo, NT) + dot(g_lo, s_hi, NT)
        now[...] = growth * now[...] + dot(b, x_hi, TN) + dot(b, x_lo, TN)

        causal = col >= row
        meets = jnp.where(causal, dot(b, c, NT), 0.0)
        mixed = jnp.zeros((size, size), F32)
        low = iota((size, lanes), 1) < HEAD_DIM
        for q in range(pairs):
            cols = slice(q * lanes, (q + 1) * lanes)
            gp = g[:, cols]
            zero = jnp.zeros_like(gp)
            stacked = jnp.concatenate([jnp.where(low, gp, zero), jnp.where(low, zero, gp)], axis=0)
            product = dot(x[:, cols], stacked, NT)
            his, los = [], []
            for e in range(2):
                h = 2 * q + e
                decay = jnp.exp(jnp.minimum(by_col[h : h + 1, :] - by_row[:, h : h + 1], 0.0))
                mixed = mixed + product[:, e * size : (e + 1) * size] * decay
                hi, lo = split2(meets * decay)
                his.append(hi)
                los.append(lo)
            inner[step, :, cols] = dot(jnp.concatenate(his, axis=1), stacked) + dot(
                jnp.concatenate(los, axis=1), stacked
            )
        mixed = jnp.where(causal, mixed, 0.0)
        hi, lo = split2(mixed)
        inner_writes[step, :, :] = dot(hi, c) + dot(lo, c)
        hi, lo = split2(mixed.T)
        reads_grad[...] = outer + dot(hi, b) + dot(lo, b)

    @pl.when(step >= count)
    def _():
        k = steps - 1 - step
        l_hi, l_lo = split2(now[...])
        x_hi, x_lo = scaled_hi[k], scaled_lo[k]
        writes_grad[...] = (
            inner_writes[k] + dot(x_hi, l_hi, NT) + dot(x_hi, l_lo, NT) + dot(x_lo, l_hi, NT)
        )
        b = writes[pl.ds(pl.multiple_of(k * size, size), size), :] if writes.shape[0] != size else writes[...]
        outer = (dot(b, l_hi) + dot(b, l_lo)) * spread2(ends[k], spread)
        values_grad[...] = (inner[k] + outer).astype(BF16)
        now[...] = jnp.exp(sums[k, 0:1, :]) * now[...] + carried[k]


def gradient_part(values, writes, reads, grads, logs, entering, leaving):
    tokens, width = values.shape
    heads = logs.shape[0]
    size = CHUNK
    count = tokens // size
    ahead = lambda k: (jnp.minimum(k, count - 1), 0)
    both = lambda k: (jnp.minimum(k, 2 * count - 1 - k), 0)
    back = lambda k: (jnp.minimum(count - 1, 2 * count - 1 - k), 0)
    whole = lambda shape: pl.BlockSpec(shape, lambda k: (0, 0))
    return pl.pallas_call(
        gradient_kernel,
        grid=(2 * count,),
        in_specs=[
            pl.BlockSpec((size, width), ahead),
            pl.BlockSpec((size, D_STATE), both),
            pl.BlockSpec((size, width), ahead),
            pl.BlockSpec((size, D_STATE), ahead),
            whole((heads, tokens)),
            whole((D_STATE, width)),
            whole((D_STATE, width)),
        ],
        out_specs=[
            pl.BlockSpec((size, width), back),
            pl.BlockSpec((size, D_STATE), back),
            pl.BlockSpec((size, D_STATE), ahead),
        ],
        out_shape=[
            jax.ShapeDtypeStruct((tokens, width), BF16),
            jax.ShapeDtypeStruct((tokens, D_STATE), F32),
            jax.ShapeDtypeStruct((tokens, D_STATE), F32),
        ],
        scratch_shapes=[
            pltpu.VMEM((D_STATE, width), F32),
            pltpu.VMEM((count, size, width), BF16),
            pltpu.VMEM((count, size, width), BF16),
            pltpu.VMEM((count, D_STATE, width), F32),
            pltpu.VMEM((count, size, width), F32),
            pltpu.VMEM((count, size, D_STATE), F32),
            pltpu.VMEM((count, size, heads), F32),
            pltpu.VMEM((count, 8, width), F32),
        ],
        compiler_params=pltpu.CompilerParams(vmem_limit_bytes=VMEM_LIMIT),
        cost_estimate=pl.CostEstimate(flops=16 * 2**30, bytes_accessed=20 * 2**20, transcendentals=0),
        name="gradient_part",
    )(values, writes, grads, reads, logs, entering, leaving)


def sum_kernel(
    writes_part, reads_part, block, writes_out, reads_out, initial_out,
    total, arrived, blocks, whole,
    send, recv, spread_send, spread_recv, near_send, near_recv,
):
    chips = blocks.shape[0]
    rows = writes_part.shape[0]
    half, quarter = rows // 2, rows // 4
    lanes = 2 * HEAD_DIM
    rank = lax.axis_index("head")
    seq = lax.axis_index("seq")
    chip, core = seq // 2, lax.rem(seq, 2)
    partner = {"seq": chip * 2 + 1 - core}
    pair_a = {"head": rank + 1 - 2 * lax.rem(rank, 2)}
    pair_b = {"head": 3 - rank}

    barrier = pltpu.get_barrier_semaphore()
    for turn in range(1, chips):
        other = lax.rem(chip + turn, chips)
        pl.semaphore_signal(barrier, inc=1, device_id={"seq": other * 2 + core}, device_id_type=MESH)
    for device in (partner, pair_a, pair_b):
        pl.semaphore_signal(barrier, inc=1, device_id=device, device_id_type=MESH)
    pl.semaphore_wait(barrier, chips + 2)

    side_a = lax.rem((rank + 1) // 2, 2)
    side_b = rank // 2
    plans = ((0, writes_part, pair_a, side_a, pair_b, side_b), (1, reads_part, pair_b, side_b, pair_a, side_a))

    def copy(k, step, source, target, device):
        c = pltpu.make_async_remote_copy(
            src_ref=source, dst_ref=target, send_sem=send.at[k, step], recv_sem=recv.at[k, step],
            device_id=device, device_id_type=MESH,
        )
        c.start()
        return c

    first = []
    for k, part, one, side_one, two, side_two in plans:
        give = pl.multiple_of((1 - side_one) * half, half)
        first.append(copy(k, 0, part.at[pl.ds(give, half), :], arrived.at[k, pl.ds(0, half), :], one))

    spreads = []
    for turn in range(1, chips):
        target = lax.rem(chip + turn, chips)
        c = pltpu.make_async_remote_copy(
            src_ref=block, dst_ref=blocks.at[chip], send_sem=spread_send.at[turn], recv_sem=spread_recv.at[chip],
            device_id={"seq": target * 2 + core}, device_id_type=MESH,
        )
        c.start()
        spreads.append(c)
    blocks[chip] = block[...]

    second = []
    for k, part, one, side_one, two, side_two in plans:
        first[k].wait()
        keep = pl.multiple_of(side_one * half, half)
        total[k, 0:half, :] = part[pl.ds(keep, half), :] + arrived[k, 0:half, :]
        give = pl.multiple_of((1 - side_two) * quarter, quarter)
        second.append(
            copy(k, 1, total.at[k, pl.ds(give, quarter), :], arrived.at[k, pl.ds(half, quarter), :], two)
        )
    third = []
    for k, part, one, side_one, two, side_two in plans:
        out = (writes_out, reads_out)[k]
        second[k].wait()
        keep = pl.multiple_of(side_two * quarter, quarter)
        spot = pl.ds(pl.multiple_of(side_one * half + side_two * quarter, quarter), quarter)
        out[spot, :] = total[k, pl.ds(keep, quarter), :] + arrived[k, pl.ds(half, quarter), :]
        third.append(copy(k, 2, out.at[spot, :], out.at[spot, :], two))
    fourth = []
    for k, part, one, side_one, two, side_two in plans:
        out = (writes_out, reads_out)[k]
        third[k].wait()
        spot = pl.ds(pl.multiple_of(side_one * half, half), half)
        fourth.append(copy(k, 3, out.at[spot, :], out.at[spot, :], one))

    for turn in range(1, chips):
        source = lax.rem(chip + turn, chips)
        pltpu.make_async_remote_copy(
            src_ref=block, dst_ref=blocks.at[source], send_sem=spread_send.at[turn], recv_sem=spread_recv.at[source],
            device_id={"seq": source * 2 + core}, device_id_type=MESH,
        ).wait_recv()
    near = pltpu.make_async_remote_copy(
        src_ref=blocks, dst_ref=whole.at[core], send_sem=near_send, recv_sem=near_recv,
        device_id=partner, device_id_type=MESH,
    )
    near.start()
    whole[core] = blocks[...]
    near.wait()
    for k in range(chips):
        both = jnp.concatenate([whole[0, k], whole[1, k]], axis=0)
        turned = both.T
        for e in range(2):
            for p in range(HEAD_DIM):
                initial_out[2 * k + e : 2 * k + e + 1, p * D_STATE : (p + 1) * D_STATE] = turned[
                    e * HEAD_DIM + p : e * HEAD_DIM + p + 1, :
                ]
    for c in spreads:
        c.wait_send()
    for c in fourth:
        c.wait()


def sum_part(writes_part, reads_part, block, chips):
    rows = writes_part.shape[0]
    half, quarter = rows // 2, rows // 4
    vmem = pl.BlockSpec(memory_space=pltpu.VMEM)
    dma = pltpu.SemaphoreType.DMA
    return pl.pallas_call(
        sum_kernel,
        in_specs=[vmem] * 3,
        out_specs=[vmem] * 3,
        out_shape=[
            jax.ShapeDtypeStruct((rows, D_STATE), F32),
            jax.ShapeDtypeStruct((rows, D_STATE), F32),
            jax.ShapeDtypeStruct((2 * chips, HEAD_DIM * D_STATE), F32),
        ],
        scratch_shapes=[
            pltpu.VMEM((2, half, D_STATE), F32),
            pltpu.VMEM((2, half + quarter, D_STATE), F32),
            pltpu.VMEM((chips,) + block.shape, F32),
            pltpu.VMEM((2, chips) + block.shape, F32),
            dma((2, 4)), dma((2, 4)), dma((chips,)), dma((chips,)), dma, dma,
        ],
        compiler_params=pltpu.CompilerParams(collective_id=1, has_side_effects=True, vmem_limit_bytes=VMEM_LIMIT),
        cost_estimate=pl.CostEstimate(flops=2**22, bytes_accessed=5 * 2**20, transcendentals=0),
        name="sum_part",
    )(writes_part, reads_part, block)


def per_device(chips, values, writes, reads, out_grad, log_decay, starting_head_state):
    seq = lax.axis_index("seq")
    chip, core = seq // 2, lax.rem(seq, 2)
    half = D_STATE // 2
    state, adjoint, total = local_part(values, writes, reads, out_grad, log_decay)
    start = lax.dynamic_slice(starting_head_state, (2 * chip, 0), (2, HEAD_DIM * D_STATE))
    start = start.reshape(2 * HEAD_DIM, D_STATE).T
    start = lax.dynamic_slice(start, (core * half, 0), (half, 2 * HEAD_DIM))
    entering, leaving, block = scan_part(state, adjoint, total, start, chips)
    values_grad, writes_local, reads_local = gradient_part(
        values, writes, reads, out_grad, log_decay, entering, leaving
    )
    writes_grad, reads_grad, initial_grad = sum_part(writes_local, reads_local, block, chips)
    return (values_grad, writes_grad, reads_grad, initial_grad)


def solution(mesh):
    in_specs = (
        P("seq", "head"),
        P("seq", None),
        P("seq", None),
        P("seq", "head"),
        P("head", "seq"),
        P("head", None),
    )
    out_specs = (P("seq", "head"), P("seq", None), P("seq", None), P("head", None))
    chips = mesh.shape["seq"] // 2
    return jax.shard_map(
        functools.partial(per_device, chips), mesh=mesh, in_specs=in_specs, out_specs=out_specs, check_vma=False
    )
```

time: 547 us -> 137 us (0.25); the launches traced: 540 us -> 137 us
  waiting for transfers between devices: 199 us -> 0 us
  matrix products: 137 us -> 0 us
  Pallas kernels: 0 us -> 128 us
  blocking collectives: 70.5 us -> 0 us
  other arithmetic: 67.2 us -> 0 us
  local copies, waits for them, and re-layouts: 48.8 us -> 8.07 us
  between operations: 15.3 us -> 0.69 us
    psum x2 -> x0, waiting for transfers between devices: 170 us -> none  [the longest x1 122 us: per_device(): initial_grad = lax.psum(jnp.exp(prefix_log) * local_adjoint, 'seq')]
    dot_general x20 -> x0, matrix products: 137 us -> none  [the longest x2 45.4 us: per_device(): jnp.einsum('hsi,shp->ihp', intersections[None] * decay_mask, grads_wide,...]
    pallas_call x0 -> x4, Pallas kernels: none -> 128 us  [the longest x1 49.1 us: scan_part(): pl.pallas_call(scan_kernel, in_specs=[vmem] * 4, out_specs=[vmem] * 3, ou...]
    unnamed x1 -> x0, blocking collectives: 70.5 us -> none
    add x32 -> x0, other arithmetic: 47 us -> none  [the longest x31 46.8 us: backward_join(): return (earlier[0] + latter[0], latter[1] + jnp.exp(latter[0]) * earlier[1])]
    all_gather x2 -> x0, waiting for transfers between devices: 28.4 us -> none  [carried_in(): gathered = jax.tree.map(lambda a: lax.all_gather(a, axis), part)]
    slice x5 -> x0, local copies, waits for them, and re-layouts: 18.5 us -> none  [the longest x2 9.48 us: per_device(): lax.slice_in_dim(out_grad, first_row, first_row + block_size)]
    mul x4 -> x0, other arithmetic: 9.83 us -> none  [the longest x1 4.25 us: per_device(): rescaled_quantities = values_wide * to_end]
  transfers between devices with their start and end apart: 4 -> 0, of which waited for: 3 -> 0; matrix products, arithmetic and copies ran while one was open for 36% -> 0% of each run, Pallas kernels for 0% -> 0%
where the time goes in v1:
time: 137 us
  Pallas kernels  128 us (93%)
  local copies, waits for them, and re-layouts  8.07 us (6%)
    pallas_call x1, Pallas kernels, scan_part(): pl.pallas_call(scan_kernel, in_specs=[vmem] * 4, out_specs=[vmem] * 3, ou...  49.1 us
    pallas_call x1, Pallas kernels, gradient_part(): pl.pallas_call(gradient_kernel, grid=(2 * count,), in_specs=[pl.BlockSpec...  36.3 us
    pallas_call x1, Pallas kernels, sum_part(): pl.pallas_call(sum_kernel, in_specs=[vmem] * 3, out_specs=[vmem] * 3, out...  31.6 us
    pallas_call x1, Pallas kernels, local_part(): pl.pallas_call(local_kernel, grid=(tokens // size,), in_specs=[wide, thin...  11 us
    unnamed x6, local copies, waits for them, and re-layouts  7.91 us

profile of v1, /device:TPU:0, one launch (start us, length us, event | category | flops | bytes accessed | tf_op | source)
XLA Modules:
  0.0 136.9 jit_solution(12788901036819811275)
XLA Ops:
  0.6 0.0 copy-start
  0.7 1.2 copy-done
  1.9 0.1 reshape.11
  2.0 0.1 constant_dynamic-slice_fusion
  2.0 0.7 copy.11
  2.7 11.0 %local_part.1 = (f32[128,2048]{1,0:T(8,128)}, f32[128,2048]{1,0:T(8,128)}, f32[8,2048]{1,0:T(8,128)}) custom-call(bf16[1024,2048]{1,0:T(8,128)(2,1)} %values.3, bf16[1024,128]{1,0:T(8,128)(2,1)} %writes.3, bf16[1024,2048]{1,0:T(8,128)(2,1)} %grads.3, bf16[1024,128]{1,0:T(8,128)(2,1)} %reads.3, f32[32,1024]{1,0:T(8,128)} %logs.3), custom_call_target="tpu_custom_call" | custom-call | flops 2147483648 | bytes 12582912 | tf_op jit(solution)/shard_map/local_part/pallas_call | solution.py:101
  13.8 49.1 %scan_part.1 = (f32[128,2048]{1,0:T(8,128)}, f32[128,2048]{1,0:T(8,128)}, f32[64,128]{1,0:T(8,128)}) custom-call(f32[128,2048]{1,0:T(8,128)} %get-tuple-element.16.state, f32[128,2048]{1,0:T(8,128)} %get-tuple-element.17.adjoint, f32[8,2048]{1,0:T(8,128)} %get-tuple-element.18.total, f32[64,128]{1,0:T(8,128)} %bitcast.1), custom_call_target="tpu_custom_call" | custom-call | flops 4194304 | bytes 5242880 | tf_op jit(solution)/shard_map/scan_part/pallas_call | solution.py:256
  62.9 36.3 %gradient_part.1 = (bf16[1024,2048]{1,0:T(8,128)(2,1)}, f32[1024,128]{1,0:T(8,128)}, f32[1024,128]{1,0:T(8,128)}) custom-call(bf16[1024,2048]{1,0:T(8,128)(2,1)} %values.3, bf16[1024,128]{1,0:T(8,128)(2,1)} %writes.3, bf16[1024,2048]{1,0:T(8,128)(2,1)} %grads.3, bf16[1024,128]{1,0:T(8,128)(2,1)} %reads.3, f32[32,1024]{1,0:T(8,128)} %logs.3, ...), custom_call_target="tpu_custom_call" | custom-call | flops 17179869184 | bytes 20971520 | tf_op jit(solution)/shard_map/gradient_part/pallas_call | solution.py:378
  99.2 31.6 %sum_part.1 = (f32[1024,128]{1,0:T(8,128)}, f32[1024,128]{1,0:T(8,128)}, f32[32,8192]{1,0:T(8,128)}) custom-call(f32[1024,128]{1,0:T(8,128)} %get-tuple-element.22.writes_part, f32[1024,128]{1,0:T(8,128)} %get-tuple-element.23.reads_part, f32[64,128]{1,0:T(8,128)} %get-tuple-element.24.block), custom_call_target="tpu_custom_call" | custom-call | flops 4194304 | bytes 5242880 | tf_op jit(solution)/shard_map/sum_part/pallas_call | solution.py:524
  130.9 1.9 %copy.15 = f32[1024,128]{1,0:T(8,128)} copy(f32[1024,128]{1,0:T(8,128)} %get-tuple-element.33) | data formatting | bytes 1048576
  132.7 1.9 %copy.16 = f32[1024,128]{1,0:T(8,128)} copy(f32[1024,128]{1,0:T(8,128)} %get-tuple-element.34) | data formatting | bytes 1048576
  134.6 2.3 %copy.17 = f32[32,8192]{1,0:T(8,128)} copy(f32[32,8192]{1,0:T(8,128)} %get-tuple-element.35) | data formatting | bytes 2097152
  (1 shorter events, 0.0 us)
Async XLA Ops:
  0.6 1.2 copy-start

commit v2 on v0

v2 whole, which is shorter than its diff:
```python
import functools

import jax
import jax.numpy as jnp
from jax import lax
from jax.experimental import pallas as pl
from jax.experimental.pallas import tpu as pltpu
from jax.sharding import PartitionSpec as P

HEAD_DIM = 64
D_STATE = 128
CHUNK = 128

MESH = pl.DeviceIdType.MESH
F32 = jnp.float32
BF16 = jnp.bfloat16
NN = (((1,), (0,)), ((), ()))
NT = (((1,), (1,)), ((), ()))
TN = (((0,), (0,)), ((), ()))
FUSED_LIMIT = 62 * 1024 * 1024


def dot(a, b, dims=NN):
    return lax.dot_general(a, b, dims, preferred_element_type=F32)


def split2(a):
    hi = a.astype(BF16)
    return hi, (a - hi.astype(F32)).astype(BF16)


def split3(a):
    hi = a.astype(BF16)
    rest = a - hi.astype(F32)
    mid = rest.astype(BF16)
    return hi, mid, (rest - mid.astype(F32)).astype(BF16)


def iota(shape, dim):
    return lax.broadcasted_iota(jnp.int32, shape, dim)


def spread_matrix(copies, heads):
    shape = (copies * heads, heads * HEAD_DIM)
    row = lax.rem(iota(shape, 0), heads)
    return (row == iota(shape, 1) // HEAD_DIM).astype(F32).astype(BF16)


def spread2(a, matrix):
    return dot(jnp.concatenate(split2(a), axis=1), matrix)


def fused_kernel(
    values, grads, start, writes, reads, logs,
    values_grad, writes_out, reads_out, initial_out,
    x_all, g_all, start_rows, start_block, start_turned, later, sooner, state, adjoint, total,
    near_state, near_adjoint, near_total, send_states, got_states, send_adjoints, got_adjoints,
    reply_states, came_states, reply_adjoints, came_adjoints, give_state, give_adjoint, entering, leaving,
    stacked_bf, now, scaled_hi, scaled_lo, carried, inner, ends, sums, behind, writes_part, reads_part,
    arrived, partial, block, blocks, whole,
    x_sem, g_sem, start_sem, near_send, near_recv, fs_send, fs_recv, fa_send, fa_recv,
    bs_send, bs_recv, ba_send, ba_recv, last_send, last_recv,
    sum_send, sum_recv, spread_send, spread_recv, whole_send, whole_recv, out_sem,
):
    chips = got_states.shape[0]
    half = D_STATE // 2
    lanes = 2 * HEAD_DIM
    tokens, width = x_all.shape
    heads = logs.shape[0]
    pairs = heads // 2
    size = CHUNK
    count = tokens // size
    wide = 256
    loads = tokens // wide
    seq = lax.axis_index("seq")
    rank = lax.axis_index("head")
    chip, core = seq // 2, lax.rem(seq, 2)
    is_first = core == 0
    partner = {"seq": chip * 2 + 1 - core}
    pair_a = {"head": rank + 1 - 2 * lax.rem(rank, 2)}
    pair_b = {"head": 3 - rank}
    own = pl.ds(pl.multiple_of(core * half, half), half)
    others = pl.ds(pl.multiple_of((1 - core) * half, half), half)

    def block_rows(k, n):
        return pl.ds(pl.multiple_of(k * n, n), n)

    def load(source, target, sem, k):
        rows = block_rows(k, wide)
        return pltpu.make_async_copy(source.at[rows, :], target.at[rows, :], sem.at[k])

    def remote(source, target, send, recv, device):
        return pltpu.make_async_remote_copy(
            src_ref=source, dst_ref=target, send_sem=send, recv_sem=recv, device_id=device, device_id_type=MESH
        )

    def chip_of(turn):
        return lax.rem(chip + turn, chips)

    def same_core(other):
        return {"seq": other * 2 + core}

    for k in range(loads):
        load(values, x_all, x_sem, k).start()
    for k in range(loads):
        load(grads, g_all, g_sem, k).start()
    start_copy = pltpu.make_async_copy(start.at[block_rows(chip // 4, 8), :], start_rows, start_sem)
    start_copy.start()

    barrier = pltpu.get_barrier_semaphore()
    for turn in range(1, chips):
        pl.semaphore_signal(barrier, inc=1, device_id=same_core(chip_of(turn)), device_id_type=MESH)
    for device in (partner, pair_a, pair_b):
        pl.semaphore_signal(barrier, inc=1, device_id=device, device_id_type=MESH)

    spread = spread_matrix(2, heads)

    row, col = iota((wide, wide), 0), iota((wide, wide), 1)
    after = (col > row).astype(F32).astype(BF16)
    upto_wide = (col <= row).astype(F32).astype(BF16)
    ones = jnp.ones((8, wide), BF16)
    parts = [split3(logs[:, k * wide : (k + 1) * wide]) for k in range(loads)]
    wholes = [sum(dot(ones, p, NT) for p in part) for part in parts]
    before = jnp.zeros((1, heads), F32)
    for k in range(loads):
        sooner[k * wide : (k + 1) * wide, :] = jnp.exp(sum(dot(upto_wide, p, NT) for p in parts[k]) + before)
        before = before + wholes[k][:1]
    rest = jnp.zeros((1, heads), F32)
    for k in reversed(range(loads)):
        later[k * wide : (k + 1) * wide, :] = jnp.exp(sum(dot(after, p, NT) for p in parts[k]) + rest)
        rest = rest + wholes[k][:1]
    total[...] = sum(dot(p, spread[:heads]) for p in split3(jnp.broadcast_to(before, (8, heads))))

    def local(source, target, sem, vectors, weights, result):
        def one(k, _):
            load(source, target, sem, k).wait()
            rows = block_rows(k, wide)
            hi, lo = split2(target[rows, :].astype(F32) * spread2(weights[rows, :], spread))
            v = vectors[rows, :]
            result[...] += dot(v, hi, TN) + dot(v, lo, TN)
            return 0

        return one

    state[...] = jnp.zeros_like(state)
    adjoint[...] = jnp.zeros_like(adjoint)
    lax.fori_loop(0, loads, local(values, x_all, x_sem, writes, later, state), 0)
    pl.semaphore_wait(barrier, chips + 2)
    near_total_copy = remote(total, near_total, near_send.at[0], near_recv.at[0], partner)
    near_total_copy.start()
    near_state_copy = remote(state.at[others, :], near_state, near_send.at[1], near_recv.at[1], partner)
    near_state_copy.start()
    local_adjoint = local(grads, g_all, g_sem, reads, sooner, adjoint)
    lax.fori_loop(0, loads // 2, local_adjoint, 0)

    def order(mine, near):
        return jnp.where(is_first, mine, near), jnp.where(is_first, near, mine)

    near_total_copy.wait()
    near_state_copy.wait()
    sent = []
    for turn in range(chips):
        target = chip_of(turn)
        cols = block_rows(target, lanes)
        log_first, log_second = order(total[:, cols], near_total[:, cols])
        first, second = order(state[own, cols], near_state[:, cols])
        place = got_states.at[chip] if turn == 0 else send_states.at[target]
        place[0:half, :] = jnp.exp(log_second[:1]) * first + second
        place[half:, :] = log_first + log_second
        if turn:
            copy = remote(
                send_states.at[target], got_states.at[chip], fs_send.at[turn], fs_recv.at[chip], same_core(target)
            )
            copy.start()
            sent.append(copy)
    lax.fori_loop(loads // 2, loads, local_adjoint, 0)
    near_adjoint_copy = remote(adjoint.at[others, :], near_adjoint, near_send.at[2], near_recv.at[2], partner)
    near_adjoint_copy.start()

    start_copy.wait()
    picks = [(iota((8, D_STATE), 0) == 2 * lax.rem(chip, 4) + e).astype(F32) for e in range(2)]
    for p in range(HEAD_DIM):
        lines = start_rows[:, p * D_STATE : (p + 1) * D_STATE]
        for e in range(2):
            start_block[e * HEAD_DIM + p : e * HEAD_DIM + p + 1, :] = jnp.sum(lines * picks[e], axis=0, keepdims=True)
    start_turned[...] = start_block[...].T

    now[...] = jnp.zeros_like(now)

    def forward(step, _):
        rows = block_rows(step, size)
        row, col = iota((size, size), 0), iota((size, size), 1)
        upto = (col <= row).astype(F32).astype(BF16)
        logs3 = split3(logs[:, rows])
        by_row = sum(dot(upto, p, NT) for p in logs3)
        by_col = sum(dot(p, upto, NT) for p in logs3)
        last = by_row[size - 1 :, :]
        to_end = jnp.exp(last - by_row)
        sums[step, :, :] = sum(dot(p, spread[:heads]) for p in split3(jnp.broadcast_to(last, (8, heads))))
        ends[step, :, :] = to_end
        growth = jnp.exp(sums[step, 0:1, :])
        b, c = writes[rows, :], reads[rows, :]
        x_hi, x_lo = split2(x_all[rows, :].astype(F32) * spread2(to_end, spread))
        g_hi, g_lo = split2(g_all[rows, :].astype(F32) * spread2(jnp.exp(by_row), spread))
        scaled_hi[step, :, :] = x_hi
        scaled_lo[step, :, :] = x_lo
        carried[step, :, :] = dot(jnp.concatenate([c, c], axis=0), jnp.concatenate([g_hi, g_lo], axis=0), TN)
        fresh = dot(jnp.concatenate([b, b], axis=0), jnp.concatenate([x_hi, x_lo], axis=0), TN)
        s_hi, s_lo = split2(now[...])
        outer = dot(g_hi, jnp.concatenate([s_hi, s_lo], axis=0), NT)
        outer = outer[:, :D_STATE] + outer[:, D_STATE:] + dot(g_lo, s_hi, NT)
        now[...] = growth * now[...] + fresh

        causal = col >= row
        meets = jnp.where(causal, dot(b, c, NT), 0.0)
        mixed = jnp.zeros((size, size), F32)
        low = iota((size, lanes), 1) < HEAD_DIM
        for q in range(pairs):
            cols = slice(q * lanes, (q + 1) * lanes)
            gp = g_all[rows, cols]
            zero = jnp.zeros_like(gp)
            stacked = jnp.concatenate([jnp.where(low, gp, zero), jnp.where(low, zero, gp)], axis=0)
            product = dot(x_all[rows, cols], stacked, NT)
            his, los = [], []
            for e in range(2):
                h = 2 * q + e
                decay = jnp.exp(jnp.minimum(by_col[h : h + 1, :] - by_row[:, h : h + 1], 0.0))
                mixed = mixed + product[:, e * size : (e + 1) * size] * decay
                hi, lo = split2(meets * decay)
                his.append(hi)
                los.append(lo)
            both = jnp.concatenate([jnp.concatenate(his, axis=1), jnp.concatenate(los, axis=1)], axis=0)
            both = dot(both, stacked)
            inner[step, :, cols] = both[:size] + both[size:]
        mixed = jnp.where(causal, mixed, 0.0)
        hi, lo = split2(mixed)
        writes_part[rows, :] = dot(hi, c) + dot(lo, c)
        hi, lo = split2(mixed.T)
        reads_part[rows, :] = outer + dot(hi, b) + dot(lo, b)
        return 0

    def against(hi, lo, stack):
        both = dot(hi, stack, NT)
        return both[:, :D_STATE] + both[:, D_STATE:] + dot(lo, stack[:D_STATE], NT)

    def backward(turn, _):
        k = count - 1 - turn
        rows = block_rows(k, size)
        stack = jnp.concatenate(split2(now[...]), axis=0)
        writes_part[rows, :] = writes_part[rows, :] + against(scaled_hi[k], scaled_lo[k], stack)
        b = writes[rows, :]
        outer = dot(jnp.concatenate([b, b], axis=1), stack)
        inner[k, :, :] = inner[k, :, :] + outer * spread2(ends[k], spread)
        growth = jnp.exp(sums[k, 0:1, :])
        now[...] = growth * now[...] + carried[k]
        return 0

    lax.fori_loop(0, 1, forward, 0)

    near_adjoint_copy.wait()
    for turn in range(chips):
        target = chip_of(turn)
        cols = block_rows(target, lanes)
        log_first, _ = order(total[:1, cols], near_total[:1, cols])
        first, second = order(adjoint[own, cols], near_adjoint[:, cols])
        place = got_adjoints.at[chip] if turn == 0 else send_adjoints.at[target]
        place[...] = first + jnp.exp(log_first) * second
        if turn:
            copy = remote(
                send_adjoints.at[target], got_adjoints.at[chip], fa_send.at[turn], fa_recv.at[chip], same_core(target)
            )
            copy.start()
            sent.append(copy)

    lax.fori_loop(1, 4, forward, 0)

    for turn in range(1, chips):
        source = chip_of(turn)
        remote(
            send_states.at[source], got_states.at[source], fs_send.at[turn], fs_recv.at[source], same_core(source)
        ).wait_recv()
    carry = start_turned[own, :]
    for k in range(chips):
        reply_states[k, :, :] = carry
        carry = jnp.exp(got_states[k, half : half + 1, :]) * carry + got_states[k, 0:half, :]
    for turn in range(1, chips):
        target = chip_of(turn)
        copy = remote(
            reply_states.at[target], came_states.at[chip], bs_send.at[turn], bs_recv.at[chip], same_core(target)
        )
        copy.start()
        sent.append(copy)

    lax.fori_loop(4, 7, forward, 0)

    for turn in range(1, chips):
        source = chip_of(turn)
        remote(
            send_adjoints.at[source], got_adjoints.at[source], fa_send.at[turn], fa_recv.at[source], same_core(source)
        ).wait_recv()
    carry = jnp.zeros((half, lanes), F32)
    for k in reversed(range(chips)):
        reply_adjoints[k, :, :] = carry
        carry = jnp.exp(got_states[k, half : half + 1, :]) * carry + got_adjoints[k, :, :]
    block[...] = carry
    for turn in range(1, chips):
        target = chip_of(turn)
        copy = remote(
            reply_adjoints.at[target], came_adjoints.at[chip], ba_send.at[turn], ba_recv.at[chip], same_core(target)
        )
        copy.start()
        sent.append(copy)

    lax.fori_loop(7, count, forward, 0)
    running = jnp.zeros((8, width), F32)
    for k in reversed(range(count)):
        behind[k, :, :] = jnp.exp(running)
        running = running + sums[k, :, :]
    now[...] = jnp.zeros_like(now)
    lax.fori_loop(0, count // 2, backward, 0)

    for turn in range(chips):
        source = chip_of(turn)
        if turn:
            remote(
                reply_states.at[source], came_states.at[source], bs_send.at[turn], bs_recv.at[source], same_core(source)
            ).wait_recv()
            came = came_states[source]
        else:
            came = reply_states[chip]
        cols = block_rows(source, lanes)
        log_first, _ = order(total[:1, cols], near_total[:1, cols])
        first, _ = order(state[own, cols], near_state[:, cols])
        moved = jnp.exp(log_first) * came + first
        entering[own, cols] = jnp.where(is_first, came, moved)
        give_state[:, cols] = jnp.where(is_first, moved, came)
    last_state = remote(give_state, entering.at[own, :], last_send.at[0], last_recv.at[0], partner)
    last_state.start()

    lax.fori_loop(count // 2, count, backward, 0)

    last_state.wait()
    stacked_bf[...] = jnp.concatenate(split2(entering[...]), axis=0)

    def read_incoming(k, _):
        rows = block_rows(k, wide)
        hi, lo = split2(g_all[rows, :].astype(F32) * spread2(sooner[rows, :], spread))
        reads_part[rows, :] = reads_part[rows, :] + against(hi, lo, stacked_bf[...])
        return 0

    lax.fori_loop(0, loads, read_incoming, 0)

    quarter = tokens // 4
    eighth = tokens // 8
    side_a = lax.rem((rank + 1) // 2, 2)
    side_b = rank // 2
    ways = ((pair_a, side_a, pair_b, side_b), (pair_b, side_b, pair_a, side_a))
    parts_of = (reads_part, writes_part)
    outs_of = (reads_out, writes_out)
    stages = [[None] * 8 for _ in range(2)]

    def begin(which, way, stage, source, target, device):
        index = (which * 2 + way) * 4 + stage
        copy = remote(source, target, sum_send.at[index], sum_recv.at[index], device)
        copy.start()
        stages[which][way * 4 + stage] = copy

    def advance(which, stage):
        part, out = parts_of[which], outs_of[which]
        for way, (one, side_one, two, side_two) in enumerate(ways):
            base = way * 2 * quarter
            slot = which * 2 + way
            if stage:
                stages[which][way * 4 + stage - 1].wait()
            if stage == 0:
                give = pl.multiple_of(base + (1 - side_one) * quarter, quarter)
                begin(which, way, 0, part.at[pl.ds(give, quarter), :], arrived.at[slot, pl.ds(0, quarter), :], one)
            elif stage == 1:
                keep = pl.multiple_of(base + side_one * quarter, quarter)
                partial[slot, :, :] = part[pl.ds(keep, quarter), :] + arrived[slot, 0:quarter, :]
                give = pl.multiple_of((1 - side_two) * eighth, eighth)
                begin(
                    which, way, 1, partial.at[slot, pl.ds(give, eighth), :],
                    arrived.at[slot, pl.ds(quarter, eighth), :], two,
                )
            elif stage == 2:
                keep = pl.multiple_of(side_two * eighth, eighth)
                spot = pl.ds(pl.multiple_of(base + side_one * quarter + side_two * eighth, eighth), eighth)
                out[spot, :] = partial[slot, pl.ds(keep, eighth), :] + arrived[slot, quarter : quarter + eighth, :]
                begin(which, way, 2, out.at[spot, :], out.at[spot, :], two)
            elif stage == 3:
                spot = pl.ds(pl.multiple_of(base + side_one * quarter, quarter), quarter)
                begin(which, way, 3, out.at[spot, :], out.at[spot, :], one)

    advance(0, 0)

    for turn in range(chips):
        source = chip_of(turn)
        if turn:
            remote(
                reply_adjoints.at[source], came_adjoints.at[source], ba_send.at[turn], ba_recv.at[source],
                same_core(source),
            ).wait_recv()
            came = came_adjoints[source]
        else:
            came = reply_adjoints[chip]
        cols = block_rows(source, lanes)
        _, log_second = order(total[:1, cols], near_total[:1, cols])
        _, second = order(adjoint[own, cols], near_adjoint[:, cols])
        moved = jnp.exp(log_second) * came + second
        leaving[own, cols] = jnp.where(is_first, moved, came)
        give_adjoint[:, cols] = jnp.where(is_first, came, moved)
    last_adjoint = remote(give_adjoint, leaving.at[own, :], last_send.at[1], last_recv.at[1], partner)
    last_adjoint.start()
    for turn in range(1, chips):
        target = chip_of(turn)
        copy = remote(block, blocks.at[chip], spread_send.at[turn], spread_recv.at[chip], same_core(target))
        copy.start()
        sent.append(copy)
    blocks[chip] = block[...]
    advance(0, 1)
    last_adjoint.wait()

    def write_incoming(k, _):
        rows = block_rows(k, size)
        stack = jnp.concatenate(split2(behind[k, 0:1, :] * leaving[...]), axis=0)
        writes_part[rows, :] = writes_part[rows, :] + against(scaled_hi[k], scaled_lo[k], stack)
        return 0

    def out_copy(k):
        rows = block_rows(k, size)
        return pltpu.make_async_copy(x_all.at[rows, :], values_grad.at[rows, :], out_sem.at[k])

    def value_incoming(k, _):
        rows = block_rows(k, size)
        stack = jnp.concatenate(split2(behind[k, 0:1, :] * leaving[...]), axis=0)
        b = writes[rows, :]
        outer = dot(jnp.concatenate([b, b], axis=1), stack)
        x_all[rows, :] = (inner[k, :, :] + outer * spread2(ends[k], spread)).astype(BF16)
        out_copy(k).start()
        return 0

    lax.fori_loop(0, count, write_incoming, 0)
    advance(1, 0)
    advance(0, 2)
    lax.fori_loop(0, 4, value_incoming, 0)
    advance(1, 1)
    advance(0, 3)
    lax.fori_loop(4, 6, value_incoming, 0)
    advance(1, 2)
    lax.fori_loop(6, count, value_incoming, 0)
    advance(1, 3)

    for turn in range(1, chips):
        source = chip_of(turn)
        remote(
            block, blocks.at[source], spread_send.at[turn], spread_recv.at[source], same_core(source)
        ).wait_recv()
    near_blocks = remote(blocks, whole.at[core], whole_send, whole_recv, partner)
    near_blocks.start()
    whole[core] = blocks[...]
    near_blocks.wait()
    for k in range(chips):
        turned = jnp.concatenate([whole[0, k], whole[1, k]], axis=0).T
        for e in range(2):
            for p in range(HEAD_DIM):
                initial_out[2 * k + e : 2 * k + e + 1, p * D_STATE : (p + 1) * D_STATE] = turned[
                    e * HEAD_DIM + p : e * HEAD_DIM + p + 1, :
                ]
    for copy in sent:
        copy.wait_send()
    for which in range(2):
        for way in range(2):
            stages[which][way * 4 + 3].wait()
    for k in range(count):
        out_copy(k).wait()


def fused_part(values, writes, reads, grads, logs, start, chips):
    tokens, width = values.shape
    heads = logs.shape[0]
    count = tokens // CHUNK
    loads = tokens // 256
    half = D_STATE // 2
    lanes = 2 * HEAD_DIM
    vmem = pl.BlockSpec(memory_space=pltpu.VMEM)
    hbm = pl.BlockSpec(memory_space=pl.ANY)
    dma = pltpu.SemaphoreType.DMA
    f32 = lambda *shape: pltpu.VMEM(shape, F32)
    bf16 = lambda *shape: pltpu.VMEM(shape, BF16)
    scratch = [
        bf16(tokens, width), bf16(tokens, width),
        f32(8, start.shape[1]), f32(D_STATE, lanes), f32(D_STATE, lanes),
        f32(tokens, heads), f32(tokens, heads),
        f32(D_STATE, width), f32(D_STATE, width), f32(8, width),
        f32(half, width), f32(half, width), f32(8, width),
        f32(chips, half + 8, lanes), f32(chips, half + 8, lanes),
        f32(chips, half, lanes), f32(chips, half, lanes),
        f32(chips, half, lanes), f32(chips, half, lanes),
        f32(chips, half, lanes), f32(chips, half, lanes),
        f32(half, width), f32(half, width),
        f32(D_STATE, width), f32(D_STATE, width),
        bf16(2 * D_STATE, width), f32(D_STATE, width),
        bf16(count, CHUNK, width), bf16(count, CHUNK, width),
        f32(count, D_STATE, width), f32(count, CHUNK, width),
        f32(count, CHUNK, heads), f32(count, 8, width), f32(count, 8, width),
        f32(tokens, D_STATE), f32(tokens, D_STATE),
        f32(4, tokens * 3 // 8, D_STATE), f32(4, tokens // 4, D_STATE),
        f32(half, lanes), f32(chips, half, lanes), f32(2, chips, half, lanes),
        dma((loads,)), dma((loads,)), dma, dma((3,)), dma((3,)),
        dma((chips,)), dma((chips,)), dma((chips,)), dma((chips,)),
        dma((chips,)), dma((chips,)), dma((chips,)), dma((chips,)), dma((2,)), dma((2,)),
        dma((16,)), dma((16,)), dma((chips,)), dma((chips,)), dma, dma, dma((count,)),
    ]
    return pl.pallas_call(
        fused_kernel,
        in_specs=[hbm, hbm, hbm, vmem, vmem, vmem],
        out_specs=[hbm, vmem, vmem, vmem],
        out_shape=[
            jax.ShapeDtypeStruct((tokens, width), BF16),
            jax.ShapeDtypeStruct((tokens, D_STATE), F32),
            jax.ShapeDtypeStruct((tokens, D_STATE), F32),
            jax.ShapeDtypeStruct((heads, HEAD_DIM * D_STATE), F32),
        ],
        scratch_shapes=scratch,
        compiler_params=pltpu.CompilerParams(collective_id=0, has_side_effects=True, vmem_limit_bytes=FUSED_LIMIT),
        cost_estimate=pl.CostEstimate(flops=2**34, bytes_accessed=20 * 2**20, transcendentals=0),
        name="fused_part",
    )(values, grads, start, writes, reads, logs)


def place_kernel(*refs):
    for source, target in zip(refs[:4], refs[4:]):
        target[...] = source[...]


def place_part(values_grad, writes_grad, reads_grad, initial_grad):
    tokens, width = values_grad.shape
    steps = 4
    rows = pl.BlockSpec((tokens // steps, width), lambda k: (k, 0))
    thin = pl.BlockSpec((tokens // steps, D_STATE), lambda k: (k, 0))
    cols = pl.BlockSpec((initial_grad.shape[0], initial_grad.shape[1] // steps), lambda k: (0, k))
    specs = [rows, thin, thin, cols]
    arrays = (values_grad, writes_grad, reads_grad, initial_grad)
    return pl.pallas_call(
        place_kernel,
        grid=(steps,),
        in_specs=specs,
        out_specs=specs,
        out_shape=[jax.ShapeDtypeStruct(a.shape, a.dtype) for a in arrays],
        compiler_params=pltpu.CompilerParams(vmem_limit_bytes=32 * 1024 * 1024),
        cost_estimate=pl.CostEstimate(flops=0, bytes_accessed=12 * 2**20, transcendentals=0),
        name="place_part",
    )(*arrays)


def per_device(chips, values, writes, reads, out_grad, log_decay, starting_head_state):
    return place_part(*fused_part(values, writes, reads, out_grad, log_decay, starting_head_state, chips))


def solution(mesh):
    in_specs = (
        P("seq", "head"),
        P("seq", None),
        P("seq", None),
        P("seq", "head"),
        P("head", "seq"),
        P("head", None),
    )
    out_specs = (P("seq", "head"), P("seq", None), P("seq", None), P("head", None))
    chips = mesh.shape["seq"] // 2
    return jax.shard_map(
        functools.partial(per_device, chips), mesh=mesh, in_specs=in_specs, out_specs=out_specs, check_vma=False
    )
```

time: 547 us -> 90 us (0.16); the launches traced: 540 us -> 89.4 us
  waiting for transfers between devices: 199 us -> 0 us
  matrix products: 137 us -> 0 us
  Pallas kernels: 0 us -> 83.2 us
  blocking collectives: 70.5 us -> 0 us
  other arithmetic: 67.2 us -> 0 us
  local copies, waits for them, and re-layouts: 48.8 us -> 5.49 us
  between operations: 15.3 us -> 0.65 us
    psum x2 -> x0, waiting for transfers between devices: 170 us -> none  [the longest x1 122 us: per_device(): initial_grad = lax.psum(jnp.exp(prefix_log) * local_adjoint, 'seq')]
    dot_general x20 -> x0, matrix products: 137 us -> none  [the longest x2 45.4 us: per_device(): jnp.einsum('hsi,shp->ihp', intersections[None] * decay_mask, grads_wide,...]
    pallas_call x0 -> x2, Pallas kernels: none -> 83.2 us  [the longest x1 80.2 us: fused_part(): pl.pallas_call(fused_kernel, in_specs=[hbm, hbm, hbm, vmem, vmem, vmem],...]
    unnamed x1 -> x0, blocking collectives: 70.5 us -> none
    add x32 -> x0, other arithmetic: 47 us -> none  [the longest x31 46.8 us: backward_join(): return (earlier[0] + latter[0], latter[1] + jnp.exp(latter[0]) * earlier[1])]
    all_gather x2 -> x0, waiting for transfers between devices: 28.4 us -> none  [carried_in(): gathered = jax.tree.map(lambda a: lax.all_gather(a, axis), part)]
    slice x5 -> x0, local copies, waits for them, and re-layouts: 18.5 us -> none  [the longest x2 9.48 us: per_device(): lax.slice_in_dim(out_grad, first_row, first_row + block_size)]
    unnamed x79 -> x8, local copies, waits for them, and re-layouts: 16.6 us -> 5.49 us
  transfers between devices with their start and end apart: 4 -> 0, of which waited for: 3 -> 0; matrix products, arithmetic and copies ran while one was open for 36% -> 0% of each run, Pallas kernels for 0% -> 0%
where the time goes in v2:
time: 90 us; the launch traced here: 89.4 us
  Pallas kernels  83.2 us (92%)
  local copies, waits for them, and re-layouts  5.49 us (6%)
    pallas_call x1, Pallas kernels, fused_part(): pl.pallas_call(fused_kernel, in_specs=[hbm, hbm, hbm, vmem, vmem, vmem],...  80.2 us
    unnamed x8, local copies, waits for them, and re-layouts  5.49 us
    pallas_call x1, Pallas kernels, place_part(): pl.pallas_call(place_kernel, grid=(steps,), in_specs=specs, out_specs=spe...  3.02 us

profile of v2, /device:TPU:0, one launch (start us, length us, event | category | flops | bytes accessed | tf_op | source)
XLA Modules:
  0.0 89.4 jit_solution(3659274753309143303)
XLA Ops:
  0.6 80.2 %fused_part.1 = (bf16[1024,2048]{1,0:T(8,128)(2,1)}, f32[1024,128]{1,0:T(8,128)}, f32[1024,128]{1,0:T(8,128)}, f32[32,8192]{1,0:T(8,128)}) custom-call(bf16[1024,2048]{1,0:T(8,128)(2,1)} %values.1, bf16[1024,2048]{1,0:T(8,128)(2,1)} %grads.1, f32[32,8192]{1,0:T(8,128)} %start.1, bf16[1024,128]{1,0:T(8,128)(2,1)} %writes.1, bf16[1024,128]{1,0:T(8,128)(2,1)} %reads.1, ...), custom_call_target="tpu_custom_call" | custom-call | flops 17179869184 | bytes 20971520 | tf_op jit(solution)/shard_map/fused_part/pallas_call | solution.py:515
  80.9 0.0 copy-start
  80.9 2.2 %copy-done = bf16[1024,2048]{1,0:T(8,128)(2,1)S(1)} copy-done((bf16[1024,2048]{1,0:T(8,128)(2,1)S(1)}, bf16[1024,2048]{1,0:T(8,128)(2,1)}, u32[]{:S(2)}) %copy-start) | copy-done | bytes 4194328
  83.1 0.0 copy-start.1
  83.1 1.2 %copy-done.1 = f32[32,8192]{1,0:T(8,128)S(1)} copy-done((f32[32,8192]{1,0:T(8,128)S(1)}, f32[32,8192]{1,0:T(8,128)}, u32[]{:S(2)}) %copy-start.1) | copy-done | bytes 1048600
  84.3 0.0 copy-start.2
  84.3 1.0 %copy-done.2 = f32[1024,128]{1,0:T(8,128)S(1)} copy-done((f32[1024,128]{1,0:T(8,128)S(1)}, f32[1024,128]{1,0:T(8,128)}, u32[]{:S(2)}) %copy-start.2) | copy-done | bytes 524312
  85.3 0.0 copy-start.3
  85.3 1.0 %copy-done.3 = f32[1024,128]{1,0:T(8,128)S(1)} copy-done((f32[1024,128]{1,0:T(8,128)S(1)}, f32[1024,128]{1,0:T(8,128)}, u32[]{:S(2)}) %copy-start.3) | copy-done | bytes 524312
  86.4 3.0 %place_part.1 = (bf16[1024,2048]{1,0:T(8,128)(2,1)}, f32[1024,128]{1,0:T(8,128)}, f32[1024,128]{1,0:T(8,128)}, f32[32,8192]{1,0:T(8,128)}) custom-call(bf16[1024,2048]{1,0:T(8,128)(2,1)S(1)} %copy-done, f32[1024,128]{1,0:T(8,128)S(1)} %copy-done.2, f32[1024,128]{1,0:T(8,128)S(1)} %copy-done.3, f32[32,8192]{1,0:T(8,128)S(1)} %copy-done.1), custom_call_target="tpu_custom_call" | custom-call | bytes 12582912 | tf_op jit(solution)/shard_map/place_part/pallas_call | solution.py:545
Async XLA Ops:
  80.9 2.2 %copy-start = (bf16[1024,2048]{1,0:T(8,128)(2,1)S(1)}, bf16[1024,2048]{1,0:T(8,128)(2,1)}, u32[]{:S(2)}) copy-start(bf16[1024,2048]{1,0:T(8,128)(2,1)} %get-tuple-element.8.refs_0_) | copy-start | bytes 12582916
  83.1 1.2 %copy-start.1 = (f32[32,8192]{1,0:T(8,128)S(1)}, f32[32,8192]{1,0:T(8,128)}, u32[]{:S(2)}) copy-start(f32[32,8192]{1,0:T(8,128)} %get-tuple-element.11.refs_3_) | copy-start | bytes 3145732
  84.3 1.0 %copy-start.2 = (f32[1024,128]{1,0:T(8,128)S(1)}, f32[1024,128]{1,0:T(8,128)}, u32[]{:S(2)}) copy-start(f32[1024,128]{1,0:T(8,128)} %get-tuple-element.9.refs_1_) | copy-start | bytes 1572868
  85.3 1.0 %copy-start.3 = (f32[1024,128]{1,0:T(8,128)S(1)}, f32[1024,128]{1,0:T(8,128)}, u32[]{:S(2)}) copy-start(f32[1024,128]{1,0:T(8,128)} %get-tuple-element.10.refs_2_) | copy-start | bytes 1572868

commit v3 on v2

v3 whole, which is shorter than its diff:
```python
import functools

import jax
import jax.numpy as jnp
from jax import lax
from jax.experimental import pallas as pl
from jax.experimental.pallas import tpu as pltpu
from jax.sharding import PartitionSpec as P

HEAD_DIM = 64
D_STATE = 128
CHUNK = 128

MESH = pl.DeviceIdType.MESH
F32 = jnp.float32
BF16 = jnp.bfloat16
NN = (((1,), (0,)), ((), ()))
NT = (((1,), (1,)), ((), ()))
TN = (((0,), (0,)), ((), ()))
FUSED_LIMIT = 62 * 1024 * 1024


def dot(a, b, dims=NN):
    return lax.dot_general(a, b, dims, preferred_element_type=F32)


def split2(a):
    hi = a.astype(BF16)
    return hi, (a - hi.astype(F32)).astype(BF16)


def split3(a):
    hi = a.astype(BF16)
    rest = a - hi.astype(F32)
    mid = rest.astype(BF16)
    return hi, mid, (rest - mid.astype(F32)).astype(BF16)


def iota(shape, dim):
    return lax.broadcasted_iota(jnp.int32, shape, dim)


def spread_matrix(copies, heads):
    shape = (copies * heads, heads * HEAD_DIM)
    row = lax.rem(iota(shape, 0), heads)
    return (row == iota(shape, 1) // HEAD_DIM).astype(F32).astype(BF16)


def spread2(a, matrix):
    return dot(jnp.concatenate(split2(a), axis=1), matrix)


AHEAD = (
    (0, 0), (2, 2), (2, 1), (1, 2), (2, 3), (3, 2), (0, 2), (2, 0),
    (1, 1), (3, 3), (1, 3), (3, 1), (0, 1), (1, 0), (0, 3), (3, 0),
)


def fused_kernel(
    values, grads, start, writes, reads, logs,
    values_grad, writes_out, reads_out, initial_out,
    x_all, g_all, start_rows, start_block, start_turned, by_rows, ends, sooner, by_cols, sums, behind,
    state, adjoint, total, near_state, near_adjoint, near_total,
    send_states, got_states, send_adjoints, got_adjoints,
    reply_states, came_states, reply_adjoints, came_adjoints, give_state, give_adjoint, entering, leaving,
    entering_stack, stacks, scaled_hi, scaled_lo, inner, writes_part, reads_part,
    arrived, partial, block, blocks, whole, turned,
    x_sem, g_sem, start_sem, near_send, near_recv, fs_send, fs_recv, fa_send, fa_recv,
    bs_send, bs_recv, ba_send, ba_recv, es_send, es_recv, la_send, la_recv,
    sum_send, sum_recv, spread_send, spread_recv, whole_send, whole_recv, out_sem,
):
    chips = got_states.shape[0]
    half = D_STATE // 2
    lanes = 2 * HEAD_DIM
    tokens, width = x_all.shape
    heads = logs.shape[0]
    pairs = heads // 2
    size = CHUNK
    count = tokens // size
    wide = 256
    seq = lax.axis_index("seq")
    rank = lax.axis_index("head")
    chip, core = seq // 2, lax.rem(seq, 2)
    is_first = core == 0
    partner = {"seq": chip * 2 + 1 - core}
    pair_a = {"head": rank + 1 - 2 * lax.rem(rank, 2)}
    pair_b = {"head": 3 - rank}
    own = pl.ds(pl.multiple_of(core * half, half), half)
    others = pl.ds(pl.multiple_of((1 - core) * half, half), half)
    sent = []

    def block_rows(k, n):
        return pl.ds(pl.multiple_of(k * n, n), n)

    def load(source, target, sem, k):
        rows = block_rows(k, size)
        return pltpu.make_async_copy(source.at[rows, :], target.at[rows, :], sem.at[k])

    def remote(source, target, send, recv, device):
        return pltpu.make_async_remote_copy(
            src_ref=source, dst_ref=target, send_sem=send, recv_sem=recv, device_id=device, device_id_type=MESH
        )

    def chip_of(turn):
        dx, dz = AHEAD[turn]
        dx = dx + core * ((4 - dx) % 4 - dx)
        dz = dz + core * ((4 - dz) % 4 - dz)
        return lax.rem(chip // 4 + dx, 4) * 4 + lax.rem(chip + dz, 4)

    def same_core(other):
        return {"seq": other * 2 + core}

    def order(mine, near):
        return jnp.where(is_first, mine, near), jnp.where(is_first, near, mine)

    for k in range(count):
        load(values, x_all, x_sem, k).start()
    for k in range(count):
        load(grads, g_all, g_sem, k).start()
    start_copy = pltpu.make_async_copy(start.at[block_rows(chip // 4, 8), :], start_rows, start_sem)
    start_copy.start()

    barrier = pltpu.get_barrier_semaphore()
    for turn in range(1, chips):
        pl.semaphore_signal(barrier, inc=1, device_id=same_core(chip_of(turn)), device_id_type=MESH)
    for device in (partner, pair_a, pair_b):
        pl.semaphore_signal(barrier, inc=1, device_id=device, device_id_type=MESH)

    spread = spread_matrix(2, heads)

    row, col = iota((size, size), 0), iota((size, size), 1)
    upto = (col <= row).astype(F32).astype(BF16)
    causal = col >= row
    low = iota((size, lanes), 1) < HEAD_DIM
    before = jnp.zeros((1, heads), F32)
    for k in range(count):
        parts = split3(logs[:, k * size : (k + 1) * size])
        by_row = sum(dot(upto, p, NT) for p in parts)
        by_cols[k] = sum(dot(p, upto, NT) for p in parts)
        by_rows[k] = by_row
        last = by_row[size - 1 :, :]
        ends[k] = jnp.exp(last - by_row)
        sooner[k] = jnp.exp(before + by_row)
        sums[k] = sum(dot(p, spread[:heads]) for p in split3(jnp.broadcast_to(last, (8, heads))))
        before = before + last
    running = jnp.zeros((8, width), F32)
    for k in reversed(range(count)):
        behind[k] = jnp.exp(running)
        running = running + sums[k]
    total[...] = running

    def twice(a):
        return jnp.concatenate([a, a], axis=0)

    def against(hi, lo, stack):
        both = dot(hi, stack, NT)
        return both[:, :D_STATE] + both[:, D_STATE:] + dot(lo, stack[:D_STATE], NT)

    def ascend(k, _):
        load(values, x_all, x_sem, k).wait()
        rows = block_rows(k, size)
        hi, lo = split2(x_all[rows, :].astype(F32) * spread2(ends[k], spread))
        scaled_hi[k] = hi
        scaled_lo[k] = lo
        fresh = dot(twice(writes[rows, :]), jnp.concatenate([hi, lo], axis=0), TN)
        now = state[...]
        stacks[k] = jnp.concatenate(split2(now), axis=0)
        state[...] = jnp.exp(sums[k, 0:1, :]) * now + fresh
        return 0

    def descend(turn, _):
        k = count - 1 - turn
        load(grads, g_all, g_sem, k).wait()
        rows = block_rows(k, size)
        hi, lo = split2(g_all[rows, :].astype(F32) * spread2(jnp.exp(by_rows[k]), spread))
        carried = dot(twice(reads[rows, :]), jnp.concatenate([hi, lo], axis=0), TN)
        reads_part[rows, :] = against(hi, lo, stacks[k])
        now = adjoint[...]
        stacks[k] = jnp.concatenate(split2(now), axis=0)
        adjoint[...] = jnp.exp(sums[k, 0:1, :]) * now + carried
        return 0

    def within(k, _):
        rows = block_rows(k, size)
        by_row, by_col = by_rows[k], by_cols[k]
        b, c = writes[rows, :], reads[rows, :]
        meets = jnp.where(causal, dot(b, c, NT), 0.0)
        mixed = jnp.zeros((size, size), F32)
        for q in range(pairs):
            cols = slice(q * lanes, (q + 1) * lanes)
            gp = g_all[rows, cols]
            zero = jnp.zeros_like(gp)
            stacked = jnp.concatenate([jnp.where(low, gp, zero), jnp.where(low, zero, gp)], axis=0)
            product = dot(x_all[rows, cols], stacked, NT)
            his, los = [], []
            for e in range(2):
                h = 2 * q + e
                decay = jnp.exp(jnp.minimum(by_col[h : h + 1, :] - by_row[:, h : h + 1], 0.0))
                mixed = mixed + product[:, e * size : (e + 1) * size] * decay
                hi, lo = split2(meets * decay)
                his.append(hi)
                los.append(lo)
            both = jnp.concatenate([jnp.concatenate(his, axis=1), jnp.concatenate(los, axis=1)], axis=0)
            both = dot(both, stacked)
            inner[k, :, cols] = both[:size] + both[size:]
        mixed = jnp.where(causal, mixed, 0.0)
        hi, lo = split2(mixed)
        writes_part[rows, :] = dot(hi, c) + dot(lo, c) + against(scaled_hi[k], scaled_lo[k], stacks[k])
        hi, lo = split2(mixed.T)
        reads_part[rows, :] = reads_part[rows, :] + dot(hi, b) + dot(lo, b)
        return 0

    state[...] = jnp.zeros_like(state)
    adjoint[...] = jnp.zeros_like(adjoint)
    lax.fori_loop(0, count, ascend, 0)
    pl.semaphore_wait(barrier, chips + 2)
    near_total_copy = remote(total, near_total, near_send.at[0], near_recv.at[0], partner)
    near_total_copy.start()
    near_state_copy = remote(state.at[others, :], near_state, near_send.at[1], near_recv.at[1], partner)
    near_state_copy.start()
    lax.fori_loop(0, 3, descend, 0)

    near_total_copy.wait()
    near_state_copy.wait()
    for turn in (*range(1, chips), 0):
        target = chip_of(turn)
        cols = block_rows(target, lanes)
        log_first, log_second = order(total[:, cols], near_total[:, cols])
        first, second = order(state[own, cols], near_state[:, cols])
        place = got_states.at[chip] if turn == 0 else send_states.at[target]
        place[0:half, :] = jnp.exp(log_second[:1]) * first + second
        place[half:, :] = log_first + log_second
        if turn:
            copy = remote(
                send_states.at[target], got_states.at[chip], fs_send.at[turn], fs_recv.at[chip], same_core(target)
            )
            copy.start()
            sent.append(copy)
    lax.fori_loop(3, count, descend, 0)
    near_adjoint_copy = remote(adjoint.at[others, :], near_adjoint, near_send.at[2], near_recv.at[2], partner)
    near_adjoint_copy.start()

    start_copy.wait()
    picks = [(iota((8, D_STATE), 0) == 2 * lax.rem(chip, 4) + e).astype(F32) for e in range(2)]
    for p in range(HEAD_DIM):
        lines = start_rows[:, p * D_STATE : (p + 1) * D_STATE]
        for e in range(2):
            start_block[e * HEAD_DIM + p : e * HEAD_DIM + p + 1, :] = jnp.sum(lines * picks[e], axis=0, keepdims=True)
    start_turned[...] = start_block[...].T

    near_adjoint_copy.wait()
    for turn in (*range(1, chips), 0):
        target = chip_of(turn)
        cols = block_rows(target, lanes)
        log_first, _ = order(total[:1, cols], near_total[:1, cols])
        first, second = order(adjoint[own, cols], near_adjoint[:, cols])
        place = got_adjoints.at[chip] if turn == 0 else send_adjoints.at[target]
        place[...] = first + jnp.exp(log_first) * second
        if turn:
            copy = remote(
                send_adjoints.at[target], got_adjoints.at[chip], fa_send.at[turn], fa_recv.at[chip], same_core(target)
            )
            copy.start()
            sent.append(copy)

    lax.fori_loop(0, 2, within, 0)

    for turn in range(1, chips):
        source = chip_of(turn)
        remote(
            send_states.at[source], got_states.at[source], fs_send.at[turn], fs_recv.at[source], same_core(source)
        ).wait_recv()
    carry = start_turned[own, :]
    for k in range(chips):
        reply_states[k] = carry
        carry = jnp.exp(got_states[k, half : half + 1, :]) * carry + got_states[k, 0:half, :]
    for turn in range(1, chips):
        target = chip_of(turn)
        copy = remote(
            reply_states.at[target], came_states.at[chip], bs_send.at[turn], bs_recv.at[chip], same_core(target)
        )
        copy.start()
        sent.append(copy)

    lax.fori_loop(2, 5, within, 0)

    for turn in range(1, chips):
        source = chip_of(turn)
        remote(
            send_adjoints.at[source], got_adjoints.at[source], fa_send.at[turn], fa_recv.at[source], same_core(source)
        ).wait_recv()
    carry = jnp.zeros((half, lanes), F32)
    for k in reversed(range(chips)):
        reply_adjoints[k] = carry
        carry = jnp.exp(got_states[k, half : half + 1, :]) * carry + got_adjoints[k]
    block[...] = carry
    for turn in range(1, chips):
        target = chip_of(turn)
        copy = remote(
            reply_adjoints.at[target], came_adjoints.at[chip], ba_send.at[turn], ba_recv.at[chip], same_core(target)
        )
        copy.start()
        sent.append(copy)

    lax.fori_loop(5, count, within, 0)

    lasts = []
    for turn in range(chips):
        source = chip_of(turn)
        if turn:
            remote(
                reply_states.at[source], came_states.at[source], bs_send.at[turn], bs_recv.at[source], same_core(source)
            ).wait_recv()
            came = came_states[source]
        else:
            came = reply_states[chip]
        cols = block_rows(source, lanes)
        log_first, _ = order(total[:1, cols], near_total[:1, cols])
        first, _ = order(state[own, cols], near_state[:, cols])
        moved = jnp.exp(log_first) * came + first
        entering[own, cols] = jnp.where(is_first, came, moved)
        give_state[:, cols] = jnp.where(is_first, moved, came)
        copy = remote(give_state.at[:, cols], entering.at[own, cols], es_send.at[source], es_recv.at[source], partner)
        copy.start()
        lasts.append(copy)
    for copy in lasts:
        copy.wait()
    entering_stack[...] = jnp.concatenate(split2(entering[...]), axis=0)

    def read_incoming(k, _):
        rows = block_rows(k, size)
        hi, lo = split2(g_all[rows, :].astype(F32) * spread2(sooner[k], spread))
        reads_part[rows, :] = reads_part[rows, :] + against(hi, lo, entering_stack[...])
        return 0

    side_a = lax.rem((rank + 1) // 2, 2)
    side_b = rank // 2
    ways = ((pair_a, side_a, pair_b, side_b), (pair_b, side_b, pair_a, side_a))
    streams = [(reads_part, reads_out, way, way * 512, 512) for way in range(2)]
    streams += [(writes_part, writes_out, k % 2, k * 256, 256) for k in range(4)]
    latest = [None] * len(streams)

    def advance(stream, stage):
        part, out, way, base, rows = streams[stream]
        one, side_one, two, side_two = ways[way]
        near, far = rows // 2, rows // 4
        if stage:
            latest[stream].wait()
        if stage == 0:
            give = pl.ds(pl.multiple_of(base + (1 - side_one) * near, near), near)
            source, target, device = part.at[give, :], arrived.at[stream, pl.ds(0, near), :], one
        elif stage == 1:
            keep = pl.ds(pl.multiple_of(base + side_one * near, near), near)
            partial[stream, 0:near, :] = part[keep, :] + arrived[stream, 0:near, :]
            give = pl.ds(pl.multiple_of((1 - side_two) * far, far), far)
            source, target, device = partial.at[stream, give, :], arrived.at[stream, pl.ds(near, far), :], two
        elif stage == 2:
            keep = pl.ds(pl.multiple_of(side_two * far, far), far)
            spot = pl.ds(pl.multiple_of(base + side_one * near + side_two * far, far), far)
            out[spot, :] = partial[stream, keep, :] + arrived[stream, near : near + far, :]
            source, target, device = out.at[spot, :], out.at[spot, :], two
        elif stage == 3:
            spot = pl.ds(pl.multiple_of(base + side_one * near, near), near)
            source, target, device = out.at[spot, :], out.at[spot, :], one
        else:
            return
        index = stream * 4 + stage
        latest[stream] = remote(source, target, sum_send.at[index], sum_recv.at[index], device)
        latest[stream].start()

    lax.fori_loop(0, count // 2, read_incoming, 0)
    advance(0, 0)
    lax.fori_loop(count // 2, count, read_incoming, 0)
    advance(1, 0)

    lasts = []
    for turn in range(chips):
        source = chip_of(turn)
        if turn:
            remote(
                reply_adjoints.at[source], came_adjoints.at[source], ba_send.at[turn], ba_recv.at[source],
                same_core(source),
            ).wait_recv()
            came = came_adjoints[source]
        else:
            came = reply_adjoints[chip]
        cols = block_rows(source, lanes)
        _, log_second = order(total[:1, cols], near_total[:1, cols])
        _, second = order(adjoint[own, cols], near_adjoint[:, cols])
        moved = jnp.exp(log_second) * came + second
        leaving[own, cols] = jnp.where(is_first, moved, came)
        give_adjoint[:, cols] = jnp.where(is_first, came, moved)
        copy = remote(give_adjoint.at[:, cols], leaving.at[own, cols], la_send.at[source], la_recv.at[source], partner)
        copy.start()
        lasts.append(copy)
    for turn in range(1, chips):
        target = chip_of(turn)
        copy = remote(block, blocks.at[chip], spread_send.at[turn], spread_recv.at[chip], same_core(target))
        copy.start()
        sent.append(copy)
    blocks[chip] = block[...]
    advance(0, 1)
    advance(1, 1)
    for copy in lasts:
        copy.wait()

    def write_incoming(k, _):
        rows = block_rows(k, size)
        stack = jnp.concatenate(split2(behind[k, 0:1, :] * leaving[...]), axis=0)
        writes_part[rows, :] = writes_part[rows, :] + against(scaled_hi[k], scaled_lo[k], stack)
        return 0

    def out_copy(k):
        rows = block_rows(k, size)
        return pltpu.make_async_copy(x_all.at[rows, :], values_grad.at[rows, :], out_sem.at[k])

    def value_incoming(k, _):
        rows = block_rows(k, size)
        mine = stacks[k, 0:D_STATE, :].astype(F32) + stacks[k, D_STATE:, :].astype(F32)
        stack = jnp.concatenate(split2(mine + behind[k, 0:1, :] * leaving[...]), axis=0)
        b = writes[rows, :]
        outer = dot(jnp.concatenate([b, b], axis=1), stack)
        x_all[rows, :] = (inner[k] + outer * spread2(ends[k], spread)).astype(BF16)
        out_copy(k).start()
        return 0

    for stream in range(4):
        lax.fori_loop(2 * stream, 2 * stream + 2, write_incoming, 0)
        advance(2 + stream, 0)
        if stream == 1:
            advance(0, 2)
            advance(1, 2)

    def value_steps(first, last):
        lax.fori_loop(first, last, value_incoming, 0)

    value_steps(0, 1)
    advance(2, 1)
    advance(3, 1)
    value_steps(1, 2)
    advance(4, 1)
    advance(5, 1)
    advance(0, 3)
    advance(1, 3)
    value_steps(2, 3)
    advance(2, 2)
    advance(3, 2)
    value_steps(3, 4)
    advance(4, 2)
    advance(5, 2)

    for turn in range(1, chips):
        source = chip_of(turn)
        remote(
            block, blocks.at[source], spread_send.at[turn], spread_recv.at[source], same_core(source)
        ).wait_recv()
    near_blocks = remote(blocks, whole.at[core], whole_send, whole_recv, partner)
    near_blocks.start()
    whole[core] = blocks[...]
    value_steps(4, 5)
    advance(2, 3)
    advance(3, 3)
    value_steps(5, 6)
    advance(4, 3)
    advance(5, 3)
    value_steps(6, count)

    near_blocks.wait()
    for k in range(chips):
        turned[k * lanes : (k + 1) * lanes, :] = jnp.concatenate([whole[0, k], whole[1, k]], axis=0).T
    for first in range(0, heads, 8):
        for p in range(HEAD_DIM):
            initial_out[first : first + 8, p * D_STATE : (p + 1) * D_STATE] = turned[
                pl.ds(first * HEAD_DIM + p, 8, stride=HEAD_DIM), :
            ]
    for copy in sent:
        copy.wait_send()
    for stream in range(len(streams)):
        advance(stream, 4)
    for k in range(count):
        out_copy(k).wait()


def fused_part(values, writes, reads, grads, logs, start, chips):
    tokens, width = values.shape
    heads = logs.shape[0]
    count = tokens // CHUNK
    half = D_STATE // 2
    lanes = 2 * HEAD_DIM
    vmem = pl.BlockSpec(memory_space=pltpu.VMEM)
    hbm = pl.BlockSpec(memory_space=pl.ANY)
    dma = pltpu.SemaphoreType.DMA
    f32 = lambda *shape: pltpu.VMEM(shape, F32)
    bf16 = lambda *shape: pltpu.VMEM(shape, BF16)
    scratch = [
        bf16(tokens, width), bf16(tokens, width),
        f32(8, start.shape[1]), f32(D_STATE, lanes), f32(D_STATE, lanes),
        f32(count, CHUNK, heads), f32(count, CHUNK, heads), f32(count, CHUNK, heads),
        f32(count, heads, CHUNK), f32(count, 8, width), f32(count, 8, width),
        f32(D_STATE, width), f32(D_STATE, width), f32(8, width),
        f32(half, width), f32(half, width), f32(8, width),
        f32(chips, half + 8, lanes), f32(chips, half + 8, lanes),
        f32(chips, half, lanes), f32(chips, half, lanes),
        f32(chips, half, lanes), f32(chips, half, lanes),
        f32(chips, half, lanes), f32(chips, half, lanes),
        f32(half, width), f32(half, width),
        f32(D_STATE, width), f32(D_STATE, width),
        bf16(2 * D_STATE, width), bf16(count, 2 * D_STATE, width),
        bf16(count, CHUNK, width), bf16(count, CHUNK, width),
        f32(count, CHUNK, width),
        f32(tokens, D_STATE), f32(tokens, D_STATE),
        f32(6, 384, D_STATE), f32(6, 256, D_STATE),
        f32(half, lanes), f32(chips, half, lanes), f32(2, chips, half, lanes),
        f32(heads * HEAD_DIM, D_STATE),
        dma((count,)), dma((count,)), dma, dma((3,)), dma((3,)),
        dma((chips,)), dma((chips,)), dma((chips,)), dma((chips,)),
        dma((chips,)), dma((chips,)), dma((chips,)), dma((chips,)),
        dma((chips,)), dma((chips,)), dma((chips,)), dma((chips,)),
        dma((24,)), dma((24,)), dma((chips,)), dma((chips,)), dma, dma, dma((count,)),
    ]
    return pl.pallas_call(
        fused_kernel,
        in_specs=[hbm, hbm, hbm, vmem, vmem, vmem],
        out_specs=[hbm, vmem, vmem, vmem],
        out_shape=[
            jax.ShapeDtypeStruct((tokens, width), BF16),
            jax.ShapeDtypeStruct((tokens, D_STATE), F32),
            jax.ShapeDtypeStruct((tokens, D_STATE), F32),
            jax.ShapeDtypeStruct((heads, HEAD_DIM * D_STATE), F32),
        ],
        scratch_shapes=scratch,
        compiler_params=pltpu.CompilerParams(collective_id=0, has_side_effects=True, vmem_limit_bytes=FUSED_LIMIT),
        cost_estimate=pl.CostEstimate(flops=2**34, bytes_accessed=20 * 2**20, transcendentals=0),
        name="fused_part",
    )(values, grads, start, writes, reads, logs)


def place_kernel(*refs):
    sources, targets, sems = refs[:4], refs[4:8], refs[8]
    copies = []
    for source, target in zip(sources, targets):
        rows = source.shape[0]
        parts = 4 if source.dtype == BF16 else 1
        for k in range(parts):
            piece = pl.ds(k * (rows // parts), rows // parts)
            copies.append(pltpu.make_async_copy(source.at[piece, :], target.at[piece, :], sems.at[len(copies)]))
    for copy in copies:
        copy.start()
    for copy in copies:
        copy.wait()


def place_part(*arrays):
    hbm = pl.BlockSpec(memory_space=pl.ANY)
    return pl.pallas_call(
        place_kernel,
        in_specs=[hbm] * 4,
        out_specs=[hbm] * 4,
        out_shape=[jax.ShapeDtypeStruct(a.shape, a.dtype) for a in arrays],
        scratch_shapes=[pltpu.SemaphoreType.DMA((7,))],
        compiler_params=pltpu.CompilerParams(vmem_limit_bytes=FUSED_LIMIT),
        cost_estimate=pl.CostEstimate(flops=0, bytes_accessed=12 * 2**20, transcendentals=0),
        name="place_part",
    )(*arrays)


def per_device(chips, values, writes, reads, out_grad, log_decay, starting_head_state):
    return place_part(*fused_part(values, writes, reads, out_grad, log_decay, starting_head_state, chips))


def solution(mesh):
    in_specs = (
        P("seq", "head"),
        P("seq", None),
        P("seq", None),
        P("seq", "head"),
        P("head", "seq"),
        P("head", None),
    )
    out_specs = (P("seq", "head"), P("seq", None), P("seq", None), P("head", None))
    chips = mesh.shape["seq"] // 2
    return jax.shard_map(
        functools.partial(per_device, chips), mesh=mesh, in_specs=in_specs, out_specs=out_specs, check_vma=False
    )
```

time: 90 us -> 270 us (3.00)
  Pallas kernels: 83.2 us -> 269 us
  local copies, waits for them, and re-layouts: 5.49 us -> 0 us
    pallas_call x1, Pallas kernels: 3.02 us -> 192 us  [place_part(): pl.pallas_call(place_kernel, in_specs=[hbm] * 4, out_specs=[hbm] * 4, out...]
    unnamed x8 -> x0, local copies, waits for them, and re-layouts: 5.49 us -> none
    pallas_call x1, Pallas kernels: 80.2 us -> 77.2 us  [fused_part(): pl.pallas_call(fused_kernel, in_specs=[hbm, hbm, hbm, vmem, vmem, vmem],...]
where the time goes in v3:
time: 270 us
  Pallas kernels  269 us (100%)
    pallas_call x1, Pallas kernels, place_part(): pl.pallas_call(place_kernel, in_specs=[hbm] * 4, out_specs=[hbm] * 4, out...  192 us
    pallas_call x1, Pallas kernels, fused_part(): pl.pallas_call(fused_kernel, in_specs=[hbm, hbm, hbm, vmem, vmem, vmem],...  77.2 us

profile of v3, /device:TPU:0, one launch (start us, length us, event | category | flops | bytes accessed | tf_op | source)
XLA Modules:
  0.0 269.8 jit_solution(3718446112011219517)
XLA Ops:
  0.6 77.2 %fused_part.1 = (bf16[1024,2048]{1,0:T(8,128)(2,1)}, f32[1024,128]{1,0:T(8,128)}, f32[1024,128]{1,0:T(8,128)}, f32[32,8192]{1,0:T(8,128)}) custom-call(bf16[1024,2048]{1,0:T(8,128)(2,1)} %values.1, bf16[1024,2048]{1,0:T(8,128)(2,1)} %grads.1, f32[32,8192]{1,0:T(8,128)} %start.1, bf16[1024,128]{1,0:T(8,128)(2,1)} %writes.1, bf16[1024,128]{1,0:T(8,128)(2,1)} %reads.1, ...), custom_call_target="tpu_custom_call" | custom-call | flops 17179869184 | bytes 20971520 | tf_op jit(solution)/shard_map/fused_part/pallas_call | solution.py:521
  77.9 191.8 %place_part.1 = (bf16[1024,2048]{1,0:T(8,128)(2,1)}, f32[1024,128]{1,0:T(8,128)}, f32[1024,128]{1,0:T(8,128)}, f32[32,8192]{1,0:T(8,128)}) custom-call(bf16[1024,2048]{1,0:T(8,128)(2,1)} %get-tuple-element.8.refs_0_, f32[1024,128]{1,0:T(8,128)} %get-tuple-element.9.refs_1_, f32[1024,128]{1,0:T(8,128)} %get-tuple-element.10.refs_2_, ...), custom_call_target="tpu_custom_call" | custom-call | bytes 12582912 | tf_op jit(solution)/shard_map/place_part/pallas_call | solution.py:555

commit v4 on v3

--- a/solution.py
+++ b/solution.py
@@ -42,8 +42,9 @@
 
 def spread_matrix(copies, heads):
     shape = (copies * heads, heads * HEAD_DIM)
-    row = lax.rem(iota(shape, 0), heads)
-    return (row == iota(shape, 1) // HEAD_DIM).astype(F32).astype(BF16)
+    low = HEAD_DIM * (iota(shape, 0) & (heads - 1))
+    col = iota(shape, 1)
+    return ((col >= low) & (col < low + HEAD_DIM)).astype(F32).astype(BF16)
 
 
 def spread2(a, matrix):
@@ -60,7 +61,7 @@
     values, grads, start, writes, reads, logs,
     values_grad, writes_out, reads_out, initial_out,
     x_all, g_all, start_rows, start_block, start_turned, by_rows, ends, sooner, by_cols, sums, behind,
-    state, adjoint, total, near_state, near_adjoint, near_total,
+    state, adjoint, now, total, near_state, near_adjoint, near_total,
     send_states, got_states, send_adjoints, got_adjoints,
     reply_states, came_states, reply_adjoints, came_adjoints, give_state, give_adjoint, entering, leaving,
     entering_stack, stacks, scaled_hi, scaled_lo, inner, writes_part, reads_part,
@@ -77,7 +78,6 @@
     pairs = heads // 2
     size = CHUNK
     count = tokens // size
-    wide = 256
     seq = lax.axis_index("seq")
     rank = lax.axis_index("head")
     chip, core = seq // 2, lax.rem(seq, 2)
@@ -132,19 +132,24 @@
     upto = (col <= row).astype(F32).astype(BF16)
     causal = col >= row
     low = iota((size, lanes), 1) < HEAD_DIM
+    parts = split3(jnp.concatenate([logs[:, k * size : (k + 1) * size] for k in range(count)], axis=0))
+    by_row_all = sum(dot(upto, p, NT) for p in parts)
+    by_col_all = sum(dot(p, upto, NT) for p in parts)
     before = jnp.zeros((1, heads), F32)
+    lasts = []
     for k in range(count):
-        parts = split3(logs[:, k * size : (k + 1) * size])
-        by_row = sum(dot(upto, p, NT) for p in parts)
-        by_cols[k] = sum(dot(p, upto, NT) for p in parts)
+        by_row = by_row_all[:, k * heads : (k + 1) * heads]
+        by_cols[k] = by_col_all[k * heads : (k + 1) * heads, :]
         by_rows[k] = by_row
         last = by_row[size - 1 :, :]
         ends[k] = jnp.exp(last - by_row)
         sooner[k] = jnp.exp(before + by_row)
-        sums[k] = sum(dot(p, spread[:heads]) for p in split3(jnp.broadcast_to(last, (8, heads))))
+        lasts.append(last)
         before = before + last
+    sums_all = sum(dot(p, spread[:heads]) for p in split3(jnp.concatenate(lasts, axis=0)))
     running = jnp.zeros((8, width), F32)
     for k in reversed(range(count)):
+        sums[k] = jnp.broadcast_to(sums_all[k : k + 1, :], (8, width))
         behind[k] = jnp.exp(running)
         running = running + sums[k]
     total[...] = running
@@ -163,9 +168,7 @@
         scaled_hi[k] = hi
         scaled_lo[k] = lo
         fresh = dot(twice(writes[rows, :]), jnp.concatenate([hi, lo], axis=0), TN)
-        now = state[...]
-        stacks[k] = jnp.concatenate(split2(now), axis=0)
-        state[...] = jnp.exp(sums[k, 0:1, :]) * now + fresh
+        state[...] = jnp.exp(sums[k, 0:1, :]) * state[...] + fresh
         return 0
 
     def descend(turn, _):
@@ -174,7 +177,6 @@
         rows = block_rows(k, size)
         hi, lo = split2(g_all[rows, :].astype(F32) * spread2(jnp.exp(by_rows[k]), spread))
         carried = dot(twice(reads[rows, :]), jnp.concatenate([hi, lo], axis=0), TN)
-        reads_part[rows, :] = against(hi, lo, stacks[k])
         now = adjoint[...]
         stacks[k] = jnp.concatenate(split2(now), axis=0)
         adjoint[...] = jnp.exp(sums[k, 0:1, :]) * now + carried
@@ -184,6 +186,10 @@
         rows = block_rows(k, size)
         by_row, by_col = by_rows[k], by_cols[k]
         b, c = writes[rows, :], reads[rows, :]
+        hi, lo = split2(g_all[rows, :].astype(F32) * spread2(jnp.exp(by_row), spread))
+        reads_outer = against(hi, lo, jnp.concatenate(split2(now[...]), axis=0))
+        fresh = dot(twice(b), jnp.concatenate([scaled_hi[k], scaled_lo[k]], axis=0), TN)
+        now[...] = jnp.exp(sums[k, 0:1, :]) * now[...] + fresh
         meets = jnp.where(causal, dot(b, c, NT), 0.0)
         mixed = jnp.zeros((size, size), F32)
         for q in range(pairs):
@@ -207,9 +213,10 @@
         hi, lo = split2(mixed)
         writes_part[rows, :] = dot(hi, c) + dot(lo, c) + against(scaled_hi[k], scaled_lo[k], stacks[k])
         hi, lo = split2(mixed.T)
-        reads_part[rows, :] = reads_part[rows, :] + dot(hi, b) + dot(lo, b)
+        reads_part[rows, :] = reads_outer + dot(hi, b) + dot(lo, b)
         return 0
 
+    now[...] = jnp.zeros_like(now)
     state[...] = jnp.zeros_like(state)
     adjoint[...] = jnp.zeros_like(adjoint)
     lax.fori_loop(0, count, ascend, 0)
@@ -497,7 +504,7 @@
         f32(8, start.shape[1]), f32(D_STATE, lanes), f32(D_STATE, lanes),
         f32(count, CHUNK, heads), f32(count, CHUNK, heads), f32(count, CHUNK, heads),
         f32(count, heads, CHUNK), f32(count, 8, width), f32(count, 8, width),
-        f32(D_STATE, width), f32(D_STATE, width), f32(8, width),
+        f32(D_STATE, width), f32(D_STATE, width), f32(D_STATE, width), f32(8, width),
         f32(half, width), f32(half, width), f32(8, width),
         f32(chips, half + 8, lanes), f32(chips, half + 8, lanes),
         f32(chips, half, lanes), f32(chips, half, lanes),
@@ -536,28 +543,20 @@
 
 
 def place_kernel(*refs):
-    sources, targets, sems = refs[:4], refs[4:8], refs[8]
-    copies = []
-    for source, target in zip(sources, targets):
-        rows = source.shape[0]
-        parts = 4 if source.dtype == BF16 else 1
-        for k in range(parts):
-            piece = pl.ds(k * (rows // parts), rows // parts)
-            copies.append(pltpu.make_async_copy(source.at[piece, :], target.at[piece, :], sems.at[len(copies)]))
-    for copy in copies:
-        copy.start()
-    for copy in copies:
-        copy.wait()
+    for source, target in zip(refs[:4], refs[4:]):
+        target[...] = source[...]
 
 
 def place_part(*arrays):
-    hbm = pl.BlockSpec(memory_space=pl.ANY)
+    steps = 8
+    rows = [pl.BlockSpec((a.shape[0] // steps, a.shape[1]), lambda k: (k, 0)) for a in arrays[:3]]
+    cols = pl.BlockSpec((arrays[3].shape[0], arrays[3].shape[1] // steps), lambda k: (0, k))
     return pl.pallas_call(
         place_kernel,
-        in_specs=[hbm] * 4,
-        out_specs=[hbm] * 4,
+        grid=(steps,),
+        in_specs=rows + [cols],
+        out_specs=rows + [cols],
         out_shape=[jax.ShapeDtypeStruct(a.shape, a.dtype) for a in arrays],
-        scratch_shapes=[pltpu.SemaphoreType.DMA((7,))],
         compiler_params=pltpu.CompilerParams(vmem_limit_bytes=FUSED_LIMIT),
         cost_estimate=pl.CostEstimate(flops=0, bytes_accessed=12 * 2**20, transcendentals=0),
         name="place_part",

time: 270 us -> 86 us (0.32)
  Pallas kernels: 269 us -> 84.9 us
    pallas_call x1, Pallas kernels: 192 us -> 7.71 us  [place_part(): pl.pallas_call(place_kernel, grid=(steps,), in_specs=rows + [cols], out_s...]
where the time goes in v4:
time: 86 us; the launch traced here: 85.7 us
  Pallas kernels  84.9 us (99%)
    pallas_call x1, Pallas kernels, fused_part(): pl.pallas_call(fused_kernel, in_specs=[hbm, hbm, hbm, vmem, vmem, vmem],...  77.2 us
    pallas_call x1, Pallas kernels, place_part(): pl.pallas_call(place_kernel, grid=(steps,), in_specs=rows + [cols], out_s...  7.71 us

profile of v4, /device:TPU:0, one launch (start us, length us, event | category | flops | bytes accessed | tf_op | source)
XLA Modules:
  0.0 85.7 jit_solution(6765414416318453938)
XLA Ops:
  0.6 77.2 %fused_part.1 = (bf16[1024,2048]{1,0:T(8,128)(2,1)}, f32[1024,128]{1,0:T(8,128)}, f32[1024,128]{1,0:T(8,128)}, f32[32,8192]{1,0:T(8,128)}) custom-call(bf16[1024,2048]{1,0:T(8,128)(2,1)} %values.1, bf16[1024,2048]{1,0:T(8,128)(2,1)} %grads.1, f32[32,8192]{1,0:T(8,128)} %start.1, bf16[1024,128]{1,0:T(8,128)(2,1)} %writes.1, bf16[1024,128]{1,0:T(8,128)(2,1)} %reads.1, ...), custom_call_target="tpu_custom_call" | custom-call | flops 17179869184 | bytes 20971520 | tf_op jit(solution)/shard_map/fused_part/pallas_call | solution.py:528
  77.9 7.7 %place_part.1 = (bf16[1024,2048]{1,0:T(8,128)(2,1)}, f32[1024,128]{1,0:T(8,128)}, f32[1024,128]{1,0:T(8,128)}, f32[32,8192]{1,0:T(8,128)}) custom-call(bf16[1024,2048]{1,0:T(8,128)(2,1)} %get-tuple-element.8.refs_0_, f32[1024,128]{1,0:T(8,128)} %get-tuple-element.9.refs_1_, f32[1024,128]{1,0:T(8,128)} %get-tuple-element.10.refs_2_, ...), custom_call_target="tpu_custom_call" | custom-call | bytes 12582912 | tf_op jit(solution)/shard_map/place_part/pallas_call | solution.py:554

commit v5 on v4

--- a/solution.py
+++ b/solution.py
@@ -61,11 +61,11 @@
     values, grads, start, writes, reads, logs,
     values_grad, writes_out, reads_out, initial_out,
     x_all, g_all, start_rows, start_block, start_turned, by_rows, ends, sooner, by_cols, sums, behind,
-    state, adjoint, now, total, near_state, near_adjoint, near_total,
+    state, adjoint, total, near_state, near_adjoint, near_total,
     send_states, got_states, send_adjoints, got_adjoints,
     reply_states, came_states, reply_adjoints, came_adjoints, give_state, give_adjoint, entering, leaving,
     entering_stack, stacks, scaled_hi, scaled_lo, inner, writes_part, reads_part,
-    arrived, partial, block, blocks, whole, turned,
+    arrived, partial, landed, block, blocks, whole, turned,
     x_sem, g_sem, start_sem, near_send, near_recv, fs_send, fs_recv, fa_send, fa_recv,
     bs_send, bs_recv, ba_send, ba_recv, es_send, es_recv, la_send, la_recv,
     sum_send, sum_recv, spread_send, spread_recv, whole_send, whole_recv, out_sem,
@@ -123,7 +123,7 @@
     barrier = pltpu.get_barrier_semaphore()
     for turn in range(1, chips):
         pl.semaphore_signal(barrier, inc=1, device_id=same_core(chip_of(turn)), device_id_type=MESH)
-    for device in (partner, pair_a, pair_b):
+    for device in (partner, pair_a, pair_b, {"head": lax.rem(rank + 2, 4)}):
         pl.semaphore_signal(barrier, inc=1, device_id=device, device_id_type=MESH)
 
     spread = spread_matrix(2, heads)
@@ -168,7 +168,9 @@
         scaled_hi[k] = hi
         scaled_lo[k] = lo
         fresh = dot(twice(writes[rows, :]), jnp.concatenate([hi, lo], axis=0), TN)
-        state[...] = jnp.exp(sums[k, 0:1, :]) * state[...] + fresh
+        now = state[...]
+        stacks[k] = jnp.concatenate(split2(now), axis=0)
+        state[...] = jnp.exp(sums[k, 0:1, :]) * now + fresh
         return 0
 
     def descend(turn, _):
@@ -177,6 +179,7 @@
         rows = block_rows(k, size)
         hi, lo = split2(g_all[rows, :].astype(F32) * spread2(jnp.exp(by_rows[k]), spread))
         carried = dot(twice(reads[rows, :]), jnp.concatenate([hi, lo], axis=0), TN)
+        reads_part[rows, :] = against(hi, lo, stacks[k])
         now = adjoint[...]
         stacks[k] = jnp.concatenate(split2(now), axis=0)
         adjoint[...] = jnp.exp(sums[k, 0:1, :]) * now + carried
@@ -186,10 +189,6 @@
         rows = block_rows(k, size)
         by_row, by_col = by_rows[k], by_cols[k]
         b, c = writes[rows, :], reads[rows, :]
-        hi, lo = split2(g_all[rows, :].astype(F32) * spread2(jnp.exp(by_row), spread))
-        reads_outer = against(hi, lo, jnp.concatenate(split2(now[...]), axis=0))
-        fresh = dot(twice(b), jnp.concatenate([scaled_hi[k], scaled_lo[k]], axis=0), TN)
-        now[...] = jnp.exp(sums[k, 0:1, :]) * now[...] + fresh
         meets = jnp.where(causal, dot(b, c, NT), 0.0)
         mixed = jnp.zeros((size, size), F32)
         for q in range(pairs):
@@ -213,14 +212,13 @@
         hi, lo = split2(mixed)
         writes_part[rows, :] = dot(hi, c) + dot(lo, c) + against(scaled_hi[k], scaled_lo[k], stacks[k])
         hi, lo = split2(mixed.T)
-        reads_part[rows, :] = reads_outer + dot(hi, b) + dot(lo, b)
+        reads_part[rows, :] = reads_part[rows, :] + dot(hi, b) + dot(lo, b)
         return 0
 
-    now[...] = jnp.zeros_like(now)
     state[...] = jnp.zeros_like(state)
     adjoint[...] = jnp.zeros_like(adjoint)
     lax.fori_loop(0, count, ascend, 0)
-    pl.semaphore_wait(barrier, chips + 2)
+    pl.semaphore_wait(barrier, chips + 3)
     near_total_copy = remote(total, near_total, near_send.at[0], near_recv.at[0], partner)
     near_total_copy.start()
     near_state_copy = remote(state.at[others, :], near_state, near_send.at[1], near_recv.at[1], partner)
@@ -344,7 +342,6 @@
     side_b = rank // 2
     ways = ((pair_a, side_a, pair_b, side_b), (pair_b, side_b, pair_a, side_a))
     streams = [(reads_part, reads_out, way, way * 512, 512) for way in range(2)]
-    streams += [(writes_part, writes_out, k % 2, k * 256, 256) for k in range(4)]
     latest = [None] * len(streams)
 
     def advance(stream, stage):
@@ -374,6 +371,32 @@
         index = stream * 4 + stage
         latest[stream] = remote(source, target, sum_send.at[index], sum_recv.at[index], device)
         latest[stream].start()
+
+    piece = tokens // 16
+
+    def piece_rows(stream, owner):
+        return pl.ds(pl.multiple_of(stream * 4 * piece + owner * piece, piece), piece)
+
+    def direct(stream, step, stage):
+        other = lax.rem(rank + step, 4)
+        index = 8 + stream * 6 + stage * 3 + step - 1
+        if stage == 0:
+            source, target = writes_part.at[piece_rows(stream, other), :], landed.at[stream, step - 1]
+        else:
+            source = target = writes_out.at[piece_rows(stream, rank), :]
+        return remote(source, target, sum_send.at[index], sum_recv.at[index], {"head": other})
+
+    def scatter(stream):
+        for step in (2, 1, 3):
+            direct(stream, step, 0).start()
+
+    def gather(stream):
+        for step in (2, 1, 3):
+            direct(stream, step, 0).wait()
+        rows = piece_rows(stream, rank)
+        writes_out[rows, :] = (writes_part[rows, :] + landed[stream, 0]) + (landed[stream, 1] + landed[stream, 2])
+        for step in (2, 1, 3):
+            direct(stream, step, 1).start()
 
     lax.fori_loop(0, count // 2, read_incoming, 0)
     advance(0, 0)
@@ -433,7 +456,7 @@
 
     for stream in range(4):
         lax.fori_loop(2 * stream, 2 * stream + 2, write_incoming, 0)
-        advance(2 + stream, 0)
+        scatter(stream)
         if stream == 1:
             advance(0, 2)
             advance(1, 2)
@@ -441,20 +464,16 @@
     def value_steps(first, last):
         lax.fori_loop(first, last, value_incoming, 0)
 
+    gather(0)
     value_steps(0, 1)
-    advance(2, 1)
-    advance(3, 1)
+    gather(1)
     value_steps(1, 2)
-    advance(4, 1)
-    advance(5, 1)
+    gather(2)
     advance(0, 3)
     advance(1, 3)
     value_steps(2, 3)
-    advance(2, 2)
-    advance(3, 2)
+    gather(3)
     value_steps(3, 4)
-    advance(4, 2)
-    advance(5, 2)
 
     for turn in range(1, chips):
         source = chip_of(turn)
@@ -464,13 +483,7 @@
     near_blocks = remote(blocks, whole.at[core], whole_send, whole_recv, partner)
     near_blocks.start()
     whole[core] = blocks[...]
-    value_steps(4, 5)
-    advance(2, 3)
-    advance(3, 3)
-    value_steps(5, 6)
-    advance(4, 3)
-    advance(5, 3)
-    value_steps(6, count)
+    value_steps(4, count)
 
     near_blocks.wait()
     for k in range(chips):
@@ -484,6 +497,9 @@
         copy.wait_send()
     for stream in range(len(streams)):
         advance(stream, 4)
+    for stream in range(4):
+        for step in range(1, 4):
+            direct(stream, step, 1).wait()
     for k in range(count):
         out_copy(k).wait()
 
@@ -504,7 +520,7 @@
         f32(8, start.shape[1]), f32(D_STATE, lanes), f32(D_STATE, lanes),
         f32(count, CHUNK, heads), f32(count, CHUNK, heads), f32(count, CHUNK, heads),
         f32(count, heads, CHUNK), f32(count, 8, width), f32(count, 8, width),
-        f32(D_STATE, width), f32(D_STATE, width), f32(D_STATE, width), f32(8, width),
+        f32(D_STATE, width), f32(D_STATE, width), f32(8, width),
         f32(half, width), f32(half, width), f32(8, width),
         f32(chips, half + 8, lanes), f32(chips, half + 8, lanes),
         f32(chips, half, lanes), f32(chips, half, lanes),
@@ -516,14 +532,14 @@
         bf16(count, CHUNK, width), bf16(count, CHUNK, width),
         f32(count, CHUNK, width),
         f32(tokens, D_STATE), f32(tokens, D_STATE),
-        f32(6, 384, D_STATE), f32(6, 256, D_STATE),
+        f32(2, 384, D_STATE), f32(2, 256, D_STATE), f32(4, 3, tokens // 16, D_STATE),
         f32(half, lanes), f32(chips, half, lanes), f32(2, chips, half, lanes),
         f32(heads * HEAD_DIM, D_STATE),
         dma((count,)), dma((count,)), dma, dma((3,)), dma((3,)),
         dma((chips,)), dma((chips,)), dma((chips,)), dma((chips,)),
         dma((chips,)), dma((chips,)), dma((chips,)), dma((chips,)),
         dma((chips,)), dma((chips,)), dma((chips,)), dma((chips,)),
-        dma((24,)), dma((24,)), dma((chips,)), dma((chips,)), dma, dma, dma((count,)),
+        dma((32,)), dma((32,)), dma((chips,)), dma((chips,)), dma, dma, dma((count,)),
     ]
     return pl.pallas_call(
         fused_kernel,
@@ -542,21 +558,36 @@
     )(values, grads, start, writes, reads, logs)
 
 
+PIECES = (8, 1, 1, 2)
+
+
 def place_kernel(*refs):
-    for source, target in zip(refs[:4], refs[4:]):
-        target[...] = source[...]
+    sources, targets, holds, in_sem, out_sem = refs[:4], refs[4:8], refs[8:12], refs[12], refs[13]
+    ins, outs = [], []
+    for source, target, hold, pieces in zip(sources, targets, holds, PIECES):
+        rows = source.shape[0] // pieces
+        for k in range(pieces):
+            piece = pl.ds(k * rows, rows)
+            ins.append(pltpu.make_async_copy(source.at[piece, :], hold.at[piece, :], in_sem.at[len(ins)]))
+            outs.append(pltpu.make_async_copy(hold.at[piece, :], target.at[piece, :], out_sem.at[len(outs)]))
+    for copy in ins:
+        copy.start()
+    for came, goes in zip(ins, outs):
+        came.wait()
+        goes.start()
+    for copy in outs:
+        copy.wait()
 
 
 def place_part(*arrays):
-    steps = 8
-    rows = [pl.BlockSpec((a.shape[0] // steps, a.shape[1]), lambda k: (k, 0)) for a in arrays[:3]]
-    cols = pl.BlockSpec((arrays[3].shape[0], arrays[3].shape[1] // steps), lambda k: (0, k))
+    hbm = pl.BlockSpec(memory_space=pl.ANY)
+    sems = pltpu.SemaphoreType.DMA((sum(PIECES),))
     return pl.pallas_call(
         place_kernel,
-        grid=(steps,),
-        in_specs=rows + [cols],
-        out_specs=rows + [cols],
+        in_specs=[hbm] * 4,
+        out_specs=[hbm] * 4,
         out_shape=[jax.ShapeDtypeStruct(a.shape, a.dtype) for a in arrays],
+        scratch_shapes=[pltpu.VMEM(a.shape, a.dtype) for a in arrays] + [sems, sems],
         compiler_params=pltpu.CompilerParams(vmem_limit_bytes=FUSED_LIMIT),
         cost_estimate=pl.CostEstimate(flops=0, bytes_accessed=12 * 2**20, transcendentals=0),
         name="place_part",

time: 86 us -> 80.6 us (0.937)
  Pallas kernels: 84.9 us -> 79.6 us
    pallas_call x1, Pallas kernels: 77.2 us -> 74.1 us  [fused_part(): pl.pallas_call(fused_kernel, in_specs=[hbm, hbm, hbm, vmem, vmem, vmem],...]
    pallas_call x1, Pallas kernels: 7.71 us -> 5.47 us  [place_part(): pl.pallas_call(place_kernel, in_specs=[hbm] * 4, out_specs=[hbm] * 4, out...]
where the time goes in v5:
time: 80.6 us; the launch traced here: 80.4 us
  Pallas kernels  79.6 us (99%)
    pallas_call x1, Pallas kernels, fused_part(): pl.pallas_call(fused_kernel, in_specs=[hbm, hbm, hbm, vmem, vmem, vmem],...  74.1 us
    pallas_call x1, Pallas kernels, place_part(): pl.pallas_call(place_kernel, in_specs=[hbm] * 4, out_specs=[hbm] * 4, out...  5.47 us

profile of v5, /device:TPU:0, one launch (start us, length us, event | category | flops | bytes accessed | tf_op | source)
XLA Modules:
  0.0 80.4 jit_solution(6880597168200801087)
XLA Ops:
  0.6 74.1 %fused_part.1 = (bf16[1024,2048]{1,0:T(8,128)(2,1)}, f32[1024,128]{1,0:T(8,128)}, f32[1024,128]{1,0:T(8,128)}, f32[32,8192]{1,0:T(8,128)}) custom-call(bf16[1024,2048]{1,0:T(8,128)(2,1)} %values.1, bf16[1024,2048]{1,0:T(8,128)(2,1)} %grads.1, f32[32,8192]{1,0:T(8,128)} %start.1, bf16[1024,128]{1,0:T(8,128)(2,1)} %writes.1, bf16[1024,128]{1,0:T(8,128)(2,1)} %reads.1, ...), custom_call_target="tpu_custom_call" | custom-call | flops 17179869184 | bytes 20971520 | tf_op jit(solution)/shard_map/fused_part/pallas_call | solution.py:544
  74.8 5.5 %place_part.1 = (bf16[1024,2048]{1,0:T(8,128)(2,1)}, f32[1024,128]{1,0:T(8,128)}, f32[1024,128]{1,0:T(8,128)}, f32[32,8192]{1,0:T(8,128)}) custom-call(bf16[1024,2048]{1,0:T(8,128)(2,1)} %get-tuple-element.8.refs_0_, f32[1024,128]{1,0:T(8,128)} %get-tuple-element.9.refs_1_, f32[1024,128]{1,0:T(8,128)} %get-tuple-element.10.refs_2_, ...), custom_call_target="tpu_custom_call" | custom-call | bytes 12582912 | tf_op jit(solution)/shard_map/place_part/pallas_call | solution.py:585

commit v6 on v5

--- a/solution.py
+++ b/solution.py
@@ -65,7 +65,7 @@
     send_states, got_states, send_adjoints, got_adjoints,
     reply_states, came_states, reply_adjoints, came_adjoints, give_state, give_adjoint, entering, leaving,
     entering_stack, stacks, scaled_hi, scaled_lo, inner, writes_part, reads_part,
-    arrived, partial, landed, block, blocks, whole, turned,
+    landed, block, blocks, whole, turned,
     x_sem, g_sem, start_sem, near_send, near_recv, fs_send, fs_recv, fa_send, fa_recv,
     bs_send, bs_recv, ba_send, ba_recv, es_send, es_recv, la_send, la_recv,
     sum_send, sum_recv, spread_send, spread_recv, whole_send, whole_recv, out_sem,
@@ -83,8 +83,6 @@
     chip, core = seq // 2, lax.rem(seq, 2)
     is_first = core == 0
     partner = {"seq": chip * 2 + 1 - core}
-    pair_a = {"head": rank + 1 - 2 * lax.rem(rank, 2)}
-    pair_b = {"head": 3 - rank}
     own = pl.ds(pl.multiple_of(core * half, half), half)
     others = pl.ds(pl.multiple_of((1 - core) * half, half), half)
     sent = []
@@ -123,7 +121,7 @@
     barrier = pltpu.get_barrier_semaphore()
     for turn in range(1, chips):
         pl.semaphore_signal(barrier, inc=1, device_id=same_core(chip_of(turn)), device_id_type=MESH)
-    for device in (partner, pair_a, pair_b, {"head": lax.rem(rank + 2, 4)}):
+    for device in (partner, *({"head": lax.rem(rank + step, 4)} for step in (1, 2, 3))):
         pl.semaphore_signal(barrier, inc=1, device_id=device, device_id_type=MESH)
 
     spread = spread_matrix(2, heads)
@@ -338,52 +336,21 @@
         reads_part[rows, :] = reads_part[rows, :] + against(hi, lo, entering_stack[...])
         return 0
 
-    side_a = lax.rem((rank + 1) // 2, 2)
-    side_b = rank // 2
-    ways = ((pair_a, side_a, pair_b, side_b), (pair_b, side_b, pair_a, side_a))
-    streams = [(reads_part, reads_out, way, way * 512, 512) for way in range(2)]
-    latest = [None] * len(streams)
-
-    def advance(stream, stage):
-        part, out, way, base, rows = streams[stream]
-        one, side_one, two, side_two = ways[way]
-        near, far = rows // 2, rows // 4
-        if stage:
-            latest[stream].wait()
-        if stage == 0:
-            give = pl.ds(pl.multiple_of(base + (1 - side_one) * near, near), near)
-            source, target, device = part.at[give, :], arrived.at[stream, pl.ds(0, near), :], one
-        elif stage == 1:
-            keep = pl.ds(pl.multiple_of(base + side_one * near, near), near)
-            partial[stream, 0:near, :] = part[keep, :] + arrived[stream, 0:near, :]
-            give = pl.ds(pl.multiple_of((1 - side_two) * far, far), far)
-            source, target, device = partial.at[stream, give, :], arrived.at[stream, pl.ds(near, far), :], two
-        elif stage == 2:
-            keep = pl.ds(pl.multiple_of(side_two * far, far), far)
-            spot = pl.ds(pl.multiple_of(base + side_one * near + side_two * far, far), far)
-            out[spot, :] = partial[stream, keep, :] + arrived[stream, near : near + far, :]
-            source, target, device = out.at[spot, :], out.at[spot, :], two
-        elif stage == 3:
-            spot = pl.ds(pl.multiple_of(base + side_one * near, near), near)
-            source, target, device = out.at[spot, :], out.at[spot, :], one
-        else:
-            return
-        index = stream * 4 + stage
-        latest[stream] = remote(source, target, sum_send.at[index], sum_recv.at[index], device)
-        latest[stream].start()
-
     piece = tokens // 16
 
+    sides = ((reads_part, reads_out), (writes_part, writes_out))
+
     def piece_rows(stream, owner):
-        return pl.ds(pl.multiple_of(stream * 4 * piece + owner * piece, piece), piece)
+        return pl.ds(pl.multiple_of((stream % 4) * 4 * piece + owner * piece, piece), piece)
 
     def direct(stream, step, stage):
         other = lax.rem(rank + step, 4)
-        index = 8 + stream * 6 + stage * 3 + step - 1
+        part, out = sides[stream // 4]
+        index = stream * 6 + stage * 3 + step - 1
         if stage == 0:
-            source, target = writes_part.at[piece_rows(stream, other), :], landed.at[stream, step - 1]
+            source, target = part.at[piece_rows(stream, other), :], landed.at[stream, step - 1]
         else:
-            source = target = writes_out.at[piece_rows(stream, rank), :]
+            source = target = out.at[piece_rows(stream, rank), :]
         return remote(source, target, sum_send.at[index], sum_recv.at[index], {"head": other})
 
     def scatter(stream):
@@ -394,14 +361,14 @@
         for step in (2, 1, 3):
             direct(stream, step, 0).wait()
         rows = piece_rows(stream, rank)
-        writes_out[rows, :] = (writes_part[rows, :] + landed[stream, 0]) + (landed[stream, 1] + landed[stream, 2])
+        part, out = sides[stream // 4]
+        out[rows, :] = (part[rows, :] + landed[stream, 0]) + (landed[stream, 1] + landed[stream, 2])
         for step in (2, 1, 3):
             direct(stream, step, 1).start()
 
-    lax.fori_loop(0, count // 2, read_incoming, 0)
-    advance(0, 0)
-    lax.fori_loop(count // 2, count, read_incoming, 0)
-    advance(1, 0)
+    for stream in range(4):
+        lax.fori_loop(2 * stream, 2 * stream + 2, read_incoming, 0)
+        scatter(stream)
 
     lasts = []
     for turn in range(chips):
@@ -429,8 +396,8 @@
         copy.start()
         sent.append(copy)
     blocks[chip] = block[...]
-    advance(0, 1)
-    advance(1, 1)
+    for stream in range(4):
+        gather(stream)
     for copy in lasts:
         copy.wait()
 
@@ -456,23 +423,18 @@
 
     for stream in range(4):
         lax.fori_loop(2 * stream, 2 * stream + 2, write_incoming, 0)
-        scatter(stream)
-        if stream == 1:
-            advance(0, 2)
-            advance(1, 2)
+        scatter(4 + stream)
 
     def value_steps(first, last):
         lax.fori_loop(first, last, value_incoming, 0)
 
-    gather(0)
+    gather(4)
     value_steps(0, 1)
-    gather(1)
+    gather(5)
     value_steps(1, 2)
-    gather(2)
-    advance(0, 3)
-    advance(1, 3)
+    gather(6)
     value_steps(2, 3)
-    gather(3)
+    gather(7)
     value_steps(3, 4)
 
     for turn in range(1, chips):
@@ -495,9 +457,7 @@
             ]
     for copy in sent:
         copy.wait_send()
-    for stream in range(len(streams)):
-        advance(stream, 4)
-    for stream in range(4):
+    for stream in range(8):
         for step in range(1, 4):
             direct(stream, step, 1).wait()
     for k in range(count):
@@ -532,14 +492,14 @@
         bf16(count, CHUNK, width), bf16(count, CHUNK, width),
         f32(count, CHUNK, width),
         f32(tokens, D_STATE), f32(tokens, D_STATE),
-        f32(2, 384, D_STATE), f32(2, 256, D_STATE), f32(4, 3, tokens // 16, D_STATE),
+        f32(8, 3, tokens // 16, D_STATE),
         f32(half, lanes), f32(chips, half, lanes), f32(2, chips, half, lanes),
         f32(heads * HEAD_DIM, D_STATE),
         dma((count,)), dma((count,)), dma, dma((3,)), dma((3,)),
         dma((chips,)), dma((chips,)), dma((chips,)), dma((chips,)),
         dma((chips,)), dma((chips,)), dma((chips,)), dma((chips,)),
         dma((chips,)), dma((chips,)), dma((chips,)), dma((chips,)),
-        dma((32,)), dma((32,)), dma((chips,)), dma((chips,)), dma, dma, dma((count,)),
+        dma((48,)), dma((48,)), dma((chips,)), dma((chips,)), dma, dma, dma((count,)),
     ]
     return pl.pallas_call(
         fused_kernel,

time: 80.6 us -> 78.9 us (0.979)
  Pallas kernels: 79.6 us -> 77.1 us
    pallas_call x1, Pallas kernels: 74.1 us -> 71.6 us  [fused_part(): pl.pallas_call(fused_kernel, in_specs=[hbm, hbm, hbm, vmem, vmem, vmem],...]
where the time goes in v6:
time: 78.9 us; the launch traced here: 77.9 us
  Pallas kernels  77.1 us (98%)
  between operations  0.8 us (1%)
    pallas_call x1, Pallas kernels, fused_part(): pl.pallas_call(fused_kernel, in_specs=[hbm, hbm, hbm, vmem, vmem, vmem],...  71.6 us
    pallas_call x1, Pallas kernels, place_part(): pl.pallas_call(place_kernel, in_specs=[hbm] * 4, out_specs=[hbm] * 4, out...  5.47 us

profile of v6, /device:TPU:0, one launch (start us, length us, event | category | flops | bytes accessed | tf_op | source)
XLA Modules:
  0.0 77.9 jit_solution(7936525631866318668)
XLA Ops:
  0.6 71.6 %fused_part.1 = (bf16[1024,2048]{1,0:T(8,128)(2,1)}, f32[1024,128]{1,0:T(8,128)}, f32[1024,128]{1,0:T(8,128)}, f32[32,8192]{1,0:T(8,128)}) custom-call(bf16[1024,2048]{1,0:T(8,128)(2,1)} %values.1, bf16[1024,2048]{1,0:T(8,128)(2,1)} %grads.1, f32[32,8192]{1,0:T(8,128)} %start.1, bf16[1024,128]{1,0:T(8,128)(2,1)} %writes.1, bf16[1024,128]{1,0:T(8,128)(2,1)} %reads.1, ...), custom_call_target="tpu_custom_call" | custom-call | flops 17179869184 | bytes 20971520 | tf_op jit(solution)/shard_map/fused_part/pallas_call | solution.py:504
  72.3 5.5 %place_part.1 = (bf16[1024,2048]{1,0:T(8,128)(2,1)}, f32[1024,128]{1,0:T(8,128)}, f32[1024,128]{1,0:T(8,128)}, f32[32,8192]{1,0:T(8,128)}) custom-call(bf16[1024,2048]{1,0:T(8,128)(2,1)} %get-tuple-element.8.refs_0_, f32[1024,128]{1,0:T(8,128)} %get-tuple-element.9.refs_1_, f32[1024,128]{1,0:T(8,128)} %get-tuple-element.10.refs_2_, ...), custom_call_target="tpu_custom_call" | custom-call | bytes 12582912 | tf_op jit(solution)/shard_map/place_part/pallas_call | solution.py:545

commit v7 on v6

--- a/solution.py
+++ b/solution.py
@@ -215,13 +215,13 @@
 
     state[...] = jnp.zeros_like(state)
     adjoint[...] = jnp.zeros_like(adjoint)
-    lax.fori_loop(0, count, ascend, 0)
+    lax.fori_loop(0, count, ascend, 0, unroll=2)
     pl.semaphore_wait(barrier, chips + 3)
     near_total_copy = remote(total, near_total, near_send.at[0], near_recv.at[0], partner)
     near_total_copy.start()
     near_state_copy = remote(state.at[others, :], near_state, near_send.at[1], near_recv.at[1], partner)
     near_state_copy.start()
-    lax.fori_loop(0, 3, descend, 0)
+    lax.fori_loop(0, 2, descend, 0, unroll=2)
 
     near_total_copy.wait()
     near_state_copy.wait()
@@ -239,7 +239,7 @@
             )
             copy.start()
             sent.append(copy)
-    lax.fori_loop(3, count, descend, 0)
+    lax.fori_loop(2, count, descend, 0, unroll=2)
     near_adjoint_copy = remote(adjoint.at[others, :], near_adjoint, near_send.at[2], near_recv.at[2], partner)
     near_adjoint_copy.start()
 
@@ -367,7 +367,7 @@
             direct(stream, step, 1).start()
 
     for stream in range(4):
-        lax.fori_loop(2 * stream, 2 * stream + 2, read_incoming, 0)
+        lax.fori_loop(2 * stream, 2 * stream + 2, read_incoming, 0, unroll=2)
         scatter(stream)
 
     lasts = []
@@ -422,7 +422,7 @@
         return 0
 
     for stream in range(4):
-        lax.fori_loop(2 * stream, 2 * stream + 2, write_incoming, 0)
+        lax.fori_loop(2 * stream, 2 * stream + 2, write_incoming, 0, unroll=2)
         scatter(4 + stream)
 
     def value_steps(first, last):

time: 78.9 us -> 78.3 us (level)
  no operation moved by 1% of the time
where the time goes in v7:
time: 78.3 us; the launch traced here: 77.4 us
  Pallas kernels  76.6 us (98%)
  between operations  0.82 us (1%)
    pallas_call x1, Pallas kernels, fused_part(): pl.pallas_call(fused_kernel, in_specs=[hbm, hbm, hbm, vmem, vmem, vmem],...  71.1 us
    pallas_call x1, Pallas kernels, place_part(): pl.pallas_call(place_kernel, in_specs=[hbm] * 4, out_specs=[hbm] * 4, out...  5.47 us

profile of v7, /device:TPU:0, one launch (start us, length us, event | category | flops | bytes accessed | tf_op | source)
XLA Modules:
  0.0 77.4 jit_solution(12628265893716128897)
XLA Ops:
  0.6 71.1 %fused_part.1 = (bf16[1024,2048]{1,0:T(8,128)(2,1)}, f32[1024,128]{1,0:T(8,128)}, f32[1024,128]{1,0:T(8,128)}, f32[32,8192]{1,0:T(8,128)}) custom-call(bf16[1024,2048]{1,0:T(8,128)(2,1)} %values.1, bf16[1024,2048]{1,0:T(8,128)(2,1)} %grads.1, f32[32,8192]{1,0:T(8,128)} %start.1, bf16[1024,128]{1,0:T(8,128)(2,1)} %writes.1, bf16[1024,128]{1,0:T(8,128)(2,1)} %reads.1, ...), custom_call_target="tpu_custom_call" | custom-call | flops 17179869184 | bytes 20971520 | tf_op jit(solution)/shard_map/fused_part/pallas_call | solution.py:504
  71.7 5.5 %place_part.1 = (bf16[1024,2048]{1,0:T(8,128)(2,1)}, f32[1024,128]{1,0:T(8,128)}, f32[1024,128]{1,0:T(8,128)}, f32[32,8192]{1,0:T(8,128)}) custom-call(bf16[1024,2048]{1,0:T(8,128)(2,1)} %get-tuple-element.8.refs_0_, f32[1024,128]{1,0:T(8,128)} %get-tuple-element.9.refs_1_, f32[1024,128]{1,0:T(8,128)} %get-tuple-element.10.refs_2_, ...), custom_call_target="tpu_custom_call" | custom-call | bytes 12582912 | tf_op jit(solution)/shard_map/place_part/pallas_call | solution.py:545
